TPU v7x, 512 devices: a whole 4x4x16 slice. The times are simulated.
512 devices in a mesh: dp: 4 (over y), row: 16 (over x, z_hi), col: 8 (over z_lo, core).
Axes of the slice: x: 4, y: 4, z: 16 (z_hi: 4, z_lo: 4; z = z_hi * 4 + z_lo), core: 2. Of those that a mesh axis runs over, the one named last changes fastest.
Arguments:
- activations: bfloat16 [7168, 6144], P(('dp', 'row'), 'col'), may hold values from -6 to 6
- cotangent: bfloat16 [7168, 12288], P(('dp', 'col'), 'row'), may hold values from -6 to 6
- preact: bfloat16 [7168, 12288], P(('dp', 'col'), 'row'), may hold values from -6 to 6
- weight: bfloat16 [6144, 12288], P('col', 'row'), may hold values from -0.078125 to 0.078125
- adapter_input_weight: bfloat16 [3, 32, 6144], P(None, None, 'col'), may hold values from -0.078125 to 0.078125
- adapter_output_weight: bfloat16 [3, 32, 12288], P(None, None, 'row'), may hold values from -1 to 1
- owner: int32 [4], replicated, may hold values from 0 to 2, as said below
Outputs:
- grad_input: bfloat16 [7168, 6144], P(('dp', 'row'), 'col')
- grad_weight: bfloat16 [6144, 12288], P('col', 'row')
- lora_in_grad: float32 [3, 32, 6144], P(None, None, 'col')
- lora_out_grad: float32 [3, 32, 12288], P(None, None, 'row')
Inputs may be any that keep to these rules, and one draw needn't show every extreme that they name: `owner`: customer of each index of dp; each of the 3 customers owns at least one index, so some own several.
All inputs are finite; a program needn't handle non-finite values.
Results may differ from a plain program's by a relative error of at most 0.024.
Values may be sent and summed in bfloat16 or wider, within the bound.
A program may use at most 64 MiB of HBM per device.

v0:
```python
import jax
import jax.numpy as jnp
from jax import lax
from jax.sharding import PartitionSpec as P

CUSTOMER_COUNT = 3


adapter_scale_factor = 2.0


def gelu_slope(value):
    return (
        0.5 * (1.0 + lax.erf(value * 0.7071067811865476))
        + value * jnp.exp(-0.5 * value * value) * 0.3989422804014327
    )


def local(
    activations, cotangent, preact, weight, adapter_input_weight, adapter_output_weight, owner
):
    client_index = owner[lax.axis_index("dp")]
    rank_down_result = lax.dynamic_index_in_dim(
        adapter_input_weight, client_index, 0, keepdims=False
    )
    rank_upward_result = lax.dynamic_index_in_dim(
        adapter_output_weight, client_index, 0, keepdims=False
    )
    wide_down_result = rank_down_result.astype(jnp.float32)
    owner_mask = (jnp.arange(CUSTOMER_COUNT) == client_index).astype(jnp.float32)
    grad_pre = (cotangent.astype(jnp.float32) * gelu_slope(preact.astype(jnp.float32))).astype(
        jnp.bfloat16
    )
    every_gradient = lax.all_gather(grad_pre, "col", axis=0, tiled=True)
    every_activation = lax.all_gather(activations, "row", axis=0, tiled=True)
    rank_everything = jnp.dot(
        every_gradient, rank_upward_result.T, preferred_element_type=jnp.float32
    )
    rank_activation = lax.psum(
        jnp.dot(every_activation, rank_down_result.T, preferred_element_type=jnp.float32).astype(
            jnp.bfloat16
        ),
        "col",
    )
    output_adapter_term = adapter_scale_factor * jnp.dot(
        rank_activation.T, every_gradient, preferred_element_type=jnp.float32
    )
    out_slots = owner_mask[:, None, None] * output_adapter_term[None]
    incomplete_term = jnp.dot(every_gradient, weight.T, preferred_element_type=jnp.float32)
    grad_input = lax.psum_scatter(
        (
            incomplete_term
            + adapter_scale_factor
            * jnp.dot(rank_everything, wide_down_result, precision=lax.Precision.HIGHEST)
        ).astype(jnp.bfloat16),
        "row",
        scatter_dimension=0,
        tiled=True,
    )
    rank_gradient = lax.psum(rank_everything.astype(jnp.bfloat16), "row")
    input_adapter_term = adapter_scale_factor * jnp.dot(
        rank_gradient.T, every_activation, preferred_element_type=jnp.float32
    )
    in_slots = owner_mask[:, None, None] * input_adapter_term[None]
    in_total, out_total = (
        lax.psum(in_slots.astype(jnp.bfloat16), "dp").astype(jnp.float32),
        lax.psum(out_slots.astype(jnp.bfloat16), "dp").astype(jnp.float32),
    )
    weight_term = lax.dot_general(
        every_activation,
        every_gradient,
        (((0,), (0,)), ((), ())),
        preferred_element_type=jnp.float32,
    )
    grad_weight = lax.psum(weight_term.astype(jnp.bfloat16), "dp")
    return (grad_input, grad_weight, in_total, out_total)


def solution(mesh):
    placed = (
        P(("dp", "row"), "col"),
        P(("dp", "col"), "row"),
        P(("dp", "col"), "row"),
        P("col", "row"),
        P(None, None, "col"),
        P(None, None, "row"),
        P(),
    )
    return jax.shard_map(
        local,
        mesh=mesh,
        in_specs=placed,
        out_specs=(
            P(("dp", "row"), "col"),
            P("col", "row"),
            P(None, None, "col"),
            P(None, None, "row"),
        ),
        check_vma=False,
    )
```

profile of v0, /device:TPU:6, one launch (start us, length us, event | category | flops | bytes accessed | tf_op | source)
XLA Modules:
  0.0 676.6 jit_solution(15331059042008291944)
XLA Ops:
  7.2 0.0 copy-start
  7.2 0.0 all-gather.3.cloned.1.call-start
  7.2 2.2 fusion.9
  9.5 0.0 all-gather.3.cloned.1.call-update
  9.5 0.0 all-gather.5.cloned.1.call-start
  9.5 0.7 all-gather.5.cloned.1.call-update
  10.2 0.0 all-reduce.5.cloned.1.call-start
  10.3 1.2 dynamic_slice.10
  13.5 0.6 compare_convert_fusion
  14.1 0.0 copy-start.2
  14.1 47.5 %all-gather.3.cloned.1.call-done = bf16[1792,768]{1,0:T(8,128)(2,1)} async-done(((bf16[224,768]{1,0:T(8,128)(2,1)}), bf16[1792,768]{1,0:T(8,128)(2,1)}) %all-gather.3.cloned.1.call-update) | async-done | bytes 2752528 | tf_op jit(solution)/shard_map/all_gather | solution.py:34
  61.7 3.4 fusion.20
  65.0 0.0 all-reduce.5.cloned.1.call-update
  65.1 0.0 all-reduce.7.cloned.1.call-start
  65.1 107.0 %all-gather.5.cloned.1.call-done = bf16[1792,768]{1,0:T(8,128)(2,1)} async-done(((bf16[112,768]{1,0:T(8,128)(2,1)}), bf16[1792,768]{1,0:T(8,128)(2,1)}) %all-gather.5.cloned.1.call-update) | async-done | bytes 2752528 | tf_op jit(solution)/shard_map/all_gather | solution.py:35
  172.1 0.0 copy-done.2
  172.1 3.4 fusion
  175.5 0.0 all-reduce.7.cloned.1.call-update
  175.5 0.0 all-reduce.9.cloned.1.call-start
  175.5 6.0 fusion.1
  181.5 189.2 %all-reduce.5.cloned.1.call-done = bf16[1792,32]{0,1:T(8,128)(2,1)} async-done(((bf16[1792,32]{0,1:T(8,128)(2,1)}), bf16[1792,32]{0,1:T(8,128)(2,1)}) %all-reduce.5.cloned.1.call-update) | async-done | bytes 114704 | tf_op jit(solution)/shard_map/psum | solution.py:60
  370.7 2.4 convolution_multiply_fusion.1
  373.1 75.0 %all-reduce.7.cloned.1.call-done = bf16[1792,32]{0,1:T(8,128)(2,1)} async-done(((bf16[1792,32]{0,1:T(8,128)(2,1)}), bf16[1792,32]{0,1:T(8,128)(2,1)}) %all-reduce.7.cloned.1.call-update) | async-done | bytes 114704 | tf_op jit(solution)/shard_map/psum | solution.py:39
  448.2 2.4 convolution_multiply_fusion
  450.6 0.8 multiply_convert_fusion
  451.5 0.0 all-reduce.9.cloned.1.call-update
  451.5 0.0 reduce-scatter.2.cloned.1.call-start
  451.5 0.0 copy-done
  451.5 4.2 fusion.21
  455.7 4.2 add_convert_fusion
  459.9 0.0 reduce-scatter.2.cloned.1.call-update
  460.0 58.0 %all-reduce.9.cloned.1.call-done = (bf16[768,768]{0,1:T(8,128)(2,1)}, bf16[3,32,768]{2,1,0:T(8,128)(2,1)}, bf16[3,32,768]{2,1,0:T(8,128)(2,1)}) async-done(((bf16[768,768]{0,1:T(8,128)(2,1)}, bf16[3,32,768]{2,1,0:T(8,128)(2,1)}, bf16[3,32,768]{2,1,0:T(8,128)(2,1)}), (bf16[768,768]{0,1:T(8,128)(2,1)}, bf16[3,32,768]{2,1,0:T(8,128)(2,1)}, bf16[3,32,768]{2,1,0:T(8,128)(2,1)})) %all-reduce.9.cloned.1.call-update) | async-done | bytes 1474576 | tf_op jit(solution)/shard_map/psum | solution.py:75
  518.0 0.0 copy-start.1
  518.0 2.4 copy.11
  520.4 1.6 convert_element_type.56
  522.0 0.0 copy-done.1
  522.0 0.7 convert_element_type.60
  522.8 147.0 %reduce-scatter.2.cloned.1.call-done = bf16[112,768]{1,0:T(8,128)(2,1)} async-done(((bf16[1792,768]{1,0:T(8,128)(2,1)}), bf16[112,768]{1,0:T(8,128)(2,1)}) %reduce-scatter.2.cloned.1.call-update) | async-done | bytes 172048 | tf_op jit(solution)/shard_map/reduce_scatter | solution.py:50
Async XLA Ops:
  7.2 444.4 %copy-start = (bf16[768,768]{1,0:T(8,128)(2,1)S(1)}, bf16[768,768]{1,0:T(8,128)(2,1)}, u32[]{:S(2)}) copy-start(bf16[768,768]{1,0:T(8,128)(2,1)} %param.10) | copy-start | bytes 3538948
  7.2 54.5 %all-gather.3.cloned.1.call-start = ((), (), s32[]{:S(2)}) async-start(), calls=%async_computation.1 | async-start | bytes 3096576 | tf_op jit(solution)/shard_map/all_gather | solution.py:34
  9.5 162.6 %all-gather.5.cloned.1.call-start = ((), (), s32[]{:S(2)}) async-start(), calls=%async_computation.3 | async-start | bytes 2924544 | tf_op jit(solution)/shard_map/all_gather | solution.py:35
  10.2 360.5 %all-reduce.5.cloned.1.call-start = ((), (), s32[]{:S(2)}) async-start(), calls=%async_computation.4 | async-start | bytes 229376 | tf_op jit(solution)/shard_map/psum | solution.py:60
  14.1 158.0 %copy-start.2 = (bf16[3,32,768]{2,1,0:T(8,128)(2,1)S(1)}, bf16[3,32,768]{2,1,0:T(8,128)(2,1)}, u32[]{:S(2)}) copy-start(bf16[3,32,768]{2,1,0:T(8,128)(2,1)} %param.11) | copy-start | bytes 442372
  65.1 383.1 %all-reduce.7.cloned.1.call-start = ((), (), s32[]{:S(2)}) async-start(), calls=%async_computation.5 | async-start | bytes 229376 | tf_op jit(solution)/shard_map/psum | solution.py:39
  175.5 342.5 %all-reduce.9.cloned.1.call-start = ((), (), s32[]{:S(2)}) async-start(), calls=%async_computation.6 | async-start | bytes 2949120 | tf_op jit(solution)/shard_map/psum | solution.py:75
  451.5 218.3 %reduce-scatter.2.cloned.1.call-start = ((), (), s32[]{:S(2)}) async-start(), calls=%async_computation.2 | async-start | bytes 2924544 | tf_op jit(solution)/shard_map/reduce_scatter | solution.py:50
  518.0 4.1 copy-start.1
Sparse Core Ops, SparseCore 0:
  10.7 50.9 all-gather.2
  64.7 107.3 all-gather.4
  175.6 195.0 all-reduce.4
  374.3 73.8 all-reduce.6
  451.6 66.3 all-reduce.8
  523.2 146.5 reduce-scatter.1
where the time goes:
time: 679 us; the launch traced here: 677 us
  waiting for transfers between devices  625 us (92%)
  matrix products  26 us (4%)
  between operations  16.1 us (2%)
    psum x1, waiting for transfers between devices, local(): rank_gradient = lax.psum(rank_everything.astype(jnp.bfloat16), 'row')  189 us
    reduce_scatter x1, waiting for transfers between devices, local(): lax.psum_scatter((incomplete_term + adapter_scale_factor * jnp.dot(rank_e...  147 us
    all_gather x1, waiting for transfers between devices, local(): every_activation = lax.all_gather(activations, 'row', axis=0, tiled=True)  107 us
    psum x1, waiting for transfers between devices, local(): lax.psum(jnp.dot(every_activation, rank_down_result.T, preferred_element_...  75 us
    psum x1, waiting for transfers between devices, local(): grad_weight = lax.psum(weight_term.astype(jnp.bfloat16), 'dp')  58 us
    all_gather x1, waiting for transfers between devices, local(): every_gradient = lax.all_gather(grad_pre, 'col', axis=0, tiled=True)  47.5 us
  transfers between devices with their start and end apart: 6, of which 6 were waited for; matrix products, arithmetic and copies ran while one was open for 4% of the time, Pallas kernels for 0%

commit v1 on v0

v1 whole, which is shorter than its diff:
```python
import functools

import jax
import jax.numpy as jnp
from jax import lax
from jax.experimental import pallas as pl
from jax.experimental.pallas import tpu as pltpu
from jax.sharding import PartitionSpec as P

MESH = pl.DeviceIdType.MESH
F32, BF16 = jnp.float32, jnp.bfloat16
SCALE = 2.0
CUSTOMERS = 3
RANK = 32


def gelu_slope(v):
    return 0.5 * (1.0 + lax.erf(v * 0.7071067811865476)) + v * jnp.exp(
        -0.5 * v * v
    ) * 0.3989422804014327


def kernel(
    x_in, cot_in, pre_in, w_in, ain_in, aout_in, owner,
    gi_out, gw_out, li_out, lo_out,
    gb, xb, cotv, prev, wv, av, bv, asel, bsel, weff, pb, rx, sz, rz, giv,
    wb, ry, ow, lis, lir, lot, lor, li2, li2r, lo2, lo2r, li3, lo3, lg, liv, lov,
    load_sem, store_sem, xz_s, xz_r, xx_s, xx_r, g_s, g_r, gk_s, gk_r, p_s, p_r, rz_s, rz_r,
    ry_s, ry_r, ag_s, ag_r, l_s, l_r,
):
    y, r, c = lax.axis_index("dp"), lax.axis_index("row"), lax.axis_index("col")
    i, j, o, k = r // 4, r % 4, c // 2, c % 2
    tok = xb.shape[1]
    blk = gb.shape[1]

    def at_x(s):
        return (y, ((i + s) % 4) * 4 + j, c)

    def at_zhi(s):
        return (y, i * 4 + (j + s) % 4, c)

    def at_zlo(s):
        return (y, r, ((o + s) % 4) * 2 + k)

    def at_y(s):
        return ((y + s) % 4, r, c)

    sibling = (y, r, o * 2 + 1 - k)

    def remote(src, dst, ss, rs, dev):
        return pltpu.make_async_remote_copy(
            src_ref=src, dst_ref=dst, send_sem=ss, recv_sem=rs, device_id=dev, device_id_type=MESH
        )

    loads = [
        pltpu.make_async_copy(a, b, load_sem.at[n])
        for n, (a, b) in enumerate(
            [(x_in, xb.at[r]), (cot_in, cotv), (pre_in, prev), (w_in, wv), (ain_in, av), (aout_in, bv)]
        )
    ]
    for cp in loads:
        cp.start()

    barrier = pltpu.get_barrier_semaphore()
    for s in range(1, 4):
        for dev in (at_x(s), at_zhi(s), at_zlo(s), at_y(s)):
            pl.semaphore_signal(barrier, inc=1, device_id=dev, device_id_type=MESH)
    pl.semaphore_signal(barrier, inc=1, device_id=sibling, device_id_type=MESH)
    pl.semaphore_wait(barrier, 13)

    def x_over_z(s):
        return remote(xb.at[r], xb.at[r], xz_s.at[s - 1], xz_r.at[s - 1], at_zhi(s))

    def x_over_x(jj, rel, s):
        row = i * 4 + jj
        return remote(xb.at[row], xb.at[row], xx_s.at[rel, s - 1], xx_r.at[rel, s - 1], at_x(s))

    loads[0].wait()
    for s in range(1, 4):
        x_over_z(s).start()
    for s in range(1, 4):
        x_over_x(j, 0, s).start()

    loads[1].wait()
    loads[2].wait()
    half = blk // 2
    for h in range(2):
        rows = pl.ds(h * half, half)
        v = prev[rows, :].astype(F32)
        gb[c, rows, :] = (cotv[rows, :].astype(F32) * gelu_slope(v)).astype(BF16)

    def g_over_z(s):
        return remote(gb.at[c], gb.at[c], g_s.at[s - 1], g_r.at[s - 1], at_zlo(s))

    def g_to_sibling(oo, rel):
        b = oo * 2 + k
        return remote(gb.at[b], gb.at[b], gk_s.at[rel], gk_r.at[rel], sibling)

    for s in range(1, 4):
        g_over_z(s).start()
    g_to_sibling(o, 0).start()

    loads[4].wait()
    loads[5].wait()
    mine = owner[y]
    a_sum = jnp.zeros(asel.shape, F32)
    b_sum = jnp.zeros(bsel.shape, F32)
    for n in range(CUSTOMERS):
        a_sum = a_sum + jnp.where(mine == n, av[n].astype(F32), 0.0)
        b_sum = b_sum + jnp.where(mine == n, bv[n].astype(F32), 0.0)
    asel[...] = a_sum.astype(BF16)
    bsel[...] = b_sum.astype(BF16)
    loads[3].wait()
    fold = lax.dot_general(asel[...], bsel[...], (((0,), (0,)), ((), ())), preferred_element_type=F32)
    weff[...] = (wv[...].astype(F32) + SCALE * fold).astype(BF16)

    def p_send(oo, kk, rel):
        rows = pl.ds(kk * blk, blk)
        return remote(
            pb.at[oo * 2 + kk], rx.at[i, rows], p_s.at[rel, kk], p_r.at[rel, kk],
            (y, oo * 4 + j, c),
        )

    def part(oo, kk):
        b = oo * 2 + kk
        pb[b] = lax.dot_general(
            gb[b], weff[...], (((1,), (1,)), ((), ())), preferred_element_type=F32
        ).astype(BF16)

        @pl.when(oo != i)
        def _():
            p_send(oo, kk, (oo - i + 4) % 4).start()

    part(o, k)
    g_to_sibling(o, 0).wait_recv()
    part(o, 1 - k)

    def step(s, carry):
        jj = (j - s + 4) % 4
        oo = (o - s + 4) % 4
        x_over_z(s).wait_recv()
        for t in range(1, 4):
            x_over_x(jj, s, t).start()
        g_over_z(s).wait_recv()
        g_to_sibling(oo, s).start()
        part(oo, k)
        g_to_sibling(oo, s).wait_recv()
        part(oo, 1 - k)
        return carry

    lax.fori_loop(1, 4, step, 0)

    for rel in range(4):
        for s in range(1, 4):
            x_over_x(j, rel, s).wait_recv()

    def ry_send(s):
        yy = (y + s) % 4
        return remote(wb.at[yy], ry.at[s - 1], ry_s.at[s - 1], ry_r.at[s - 1], at_y(s))

    width = weff.shape[0]
    xs = xb[...].reshape(16 * tok, width)
    gs = gb[...].reshape(8 * blk, width)
    for h in range(2):
        cols = width // 2
        term = lax.dot_general(
            xs[:, h * cols : (h + 1) * cols], gs, (((0,), (0,)), ((), ())), preferred_element_type=F32
        ).astype(BF16)
        wb[2 * h] = term[: cols // 2]
        wb[2 * h + 1] = term[cols // 2 :]
    for s in range(1, 4):
        ry_send(s).start()

    for rel in range(1, 4):
        for kk in range(2):
            p_send(o, kk, rel).wait_recv()
    for q in range(4):
        rows = pl.ds(q * tok, tok)
        total = pb[2 * i + q // 2, pl.ds((q % 2) * tok, tok), :].astype(F32)
        for s in range(1, 4):
            total = total + rx[(i + s) % 4, rows, :].astype(F32)
        sz[q] = total.astype(BF16)

    def rz_send(s):
        jj = (j + s) % 4
        return remote(sz.at[jj], rz.at[s - 1], rz_s.at[s - 1], rz_r.at[s - 1], at_zhi(s))

    for s in range(1, 4):
        rz_send(s).start()

    wfull = wb[...].reshape(width, width)
    lin = SCALE * lax.dot_general(bsel[...], wfull, (((1,), (1,)), ((), ())), preferred_element_type=F32)
    lout = SCALE * lax.dot_general(asel[...], wfull, (((1,), (0,)), ((), ())), preferred_element_type=F32)
    lis[...] = lin.reshape(lis.shape)
    lot[...] = lout.reshape(lot.shape)

    def li_x(s):
        return remote(lis.at[(i + s) % 4], lir.at[s - 1], l_s.at[0, s - 1], l_r.at[0, s - 1], at_x(s))

    def lo_z(s):
        return remote(lot.at[(o + s) % 4], lor.at[s - 1], l_s.at[1, s - 1], l_r.at[1, s - 1], at_zlo(s))

    def li_zhi(s):
        return remote(li2.at[j], li2.at[j], l_s.at[2, s - 1], l_r.at[2, s - 1], at_zhi(s))

    def lo_k():
        return remote(lo2, lo2r, l_s.at[3, 0], l_r.at[3, 0], sibling)

    def li_ag(s):
        return remote(li3.at[i], li3.at[i], l_s.at[4, s - 1], l_r.at[4, s - 1], at_x(s))

    def lo_ag(s):
        return remote(lo3.at[o], lo3.at[o], l_s.at[5, s - 1], l_r.at[5, s - 1], at_zlo(s))

    def lg_ag(s):
        return remote(lg.at[y], lg.at[y], l_s.at[6, s - 1], l_r.at[6, s - 1], at_y(s))

    for s in range(1, 4):
        li_x(s).start()
        lo_z(s).start()

    for s in range(1, 4):
        li_x(s).wait_recv()
    li2[j] = (lis[i] + lir[0]) + (lir[1] + lir[2])
    for s in range(1, 4):
        li_zhi(s).start()
    for s in range(1, 4):
        lo_z(s).wait_recv()
    lo2[...] = (lot[o] + lor[0]) + (lor[1] + lor[2])
    lo_k().start()

    for s in range(1, 4):
        ry_send(s).wait_recv()
    total = wb[y].astype(F32)
    for s in range(3):
        total = total + ry[s].astype(F32)
    ow[y] = total.astype(BF16)

    def ow_ag(s):
        return remote(ow.at[y], ow.at[y], ag_s.at[s - 1], ag_r.at[s - 1], at_y(s))

    for s in range(1, 4):
        ow_ag(s).start()

    for s in range(1, 4):
        li_zhi(s).wait_recv()
    li3[i] = (li2[0] + li2[1]) + (li2[2] + li2[3])
    for s in range(1, 4):
        li_ag(s).start()
    lo_k().wait_recv()
    lo3[o] = lo2[...] + lo2r[...]
    for s in range(1, 4):
        lo_ag(s).start()
    for s in range(1, 4):
        li_ag(s).wait_recv()
        lo_ag(s).wait_recv()
    lg[y, :RANK] = li3[...].reshape(RANK, width).astype(BF16)
    lg[y, RANK:] = lo3[...].reshape(RANK, width).astype(BF16)
    for s in range(1, 4):
        lg_ag(s).start()

    for s in range(1, 4):
        rz_send(s).wait_recv()
    total = sz[j].astype(F32)
    for s in range(3):
        total = total + rz[s].astype(F32)
    giv[...] = total.astype(BF16)
    gi_store = pltpu.make_async_copy(giv, gi_out, store_sem.at[0])
    gi_store.start()

    for s in range(1, 4):
        lg_ag(s).wait_recv()
    for n in range(CUSTOMERS):
        acc = jnp.zeros((2 * RANK, width), F32)
        for g in range(4):
            acc = acc + jnp.where(owner[g] == n, lg[g].astype(F32), 0.0)
        liv[n] = acc[:RANK]
        lov[n] = acc[RANK:]
    li_store = pltpu.make_async_copy(liv, li_out, store_sem.at[1])
    lo_store = pltpu.make_async_copy(lov, lo_out, store_sem.at[2])
    li_store.start()
    lo_store.start()

    for s in range(1, 4):
        ow_ag(s).wait_recv()
    gw_store = pltpu.make_async_copy(ow, gw_out, store_sem.at[3])
    gw_store.start()

    for s in range(1, 4):
        x_over_z(s).wait_send()
        g_over_z(s).wait_send()
        rz_send(s).wait_send()
        ry_send(s).wait_send()
        ow_ag(s).wait_send()
        li_x(s).wait_send()
        lo_z(s).wait_send()
        li_zhi(s).wait_send()
        li_ag(s).wait_send()
        lo_ag(s).wait_send()
        lg_ag(s).wait_send()
        for kk in range(2):
            p_send(o, kk, s).wait_send()
    for rel in range(4):
        g_to_sibling(o, rel).wait_send()
        for s in range(1, 4):
            x_over_x(j, rel, s).wait_send()
    lo_k().wait_send()
    gi_store.wait()
    li_store.wait()
    lo_store.wait()
    gw_store.wait()


def local(activations, cotangent, preact, weight, ain, aout, owner):
    tok, width = activations.shape
    blk = cotangent.shape[0]
    quarter = width // 4
    any_ = pl.BlockSpec(memory_space=pltpu.HBM)
    dma = pltpu.SemaphoreType.DMA
    v = pltpu.VMEM
    r8 = RANK // 4
    scratch = [
        v((8, blk, width), BF16),
        v((16, tok, width), BF16),
        v((blk, width), BF16),
        v((blk, width), BF16),
        v((width, width), BF16),
        v((CUSTOMERS, RANK, width), BF16),
        v((CUSTOMERS, RANK, width), BF16),
        v((RANK, width), BF16),
        v((RANK, width), BF16),
        v((width, width), BF16),
        v((8, blk, width), BF16),
        v((4, 2 * blk, width), BF16),
        v((4, tok, width), BF16),
        v((3, tok, width), BF16),
        v((tok, width), BF16),
        v((4, quarter, width), BF16),
        v((3, quarter, width), BF16),
        v((4, quarter, width), BF16),
        v((4, r8, width), F32),
        v((3, r8, width), F32),
        v((4, r8, width), F32),
        v((3, r8, width), F32),
        v((4, r8, width), F32),
        v((4, r8, width), F32),
        v((r8, width), F32),
        v((r8, width), F32),
        v((4, r8, width), F32),
        v((4, r8, width), F32),
        v((4, 2 * RANK, width), BF16),
        v((CUSTOMERS, RANK, width), F32),
        v((CUSTOMERS, RANK, width), F32),
        dma((6,)), dma((4,)),
        dma((3,)), dma((3,)), dma((4, 3)), dma((4, 3)),
        dma((3,)), dma((3,)), dma((4,)), dma((4,)),
        dma((4, 2)), dma((4, 2)), dma((3,)), dma((3,)),
        dma((3,)), dma((3,)), dma((3,)), dma((3,)),
        dma((7, 3)), dma((7, 3)),
    ]
    gi, gw, li, lo = pl.pallas_call(
        kernel,
        out_shape=(
            jax.ShapeDtypeStruct((tok, width), BF16),
            jax.ShapeDtypeStruct((4, quarter, width), BF16),
            jax.ShapeDtypeStruct((CUSTOMERS, RANK, width), F32),
            jax.ShapeDtypeStruct((CUSTOMERS, RANK, width), F32),
        ),
        in_specs=[any_] * 6 + [pl.BlockSpec(memory_space=pltpu.SMEM)],
        out_specs=[any_] * 4,
        scratch_shapes=scratch,
        compiler_params=pltpu.CompilerParams(
            collective_id=0, has_side_effects=True, vmem_limit_bytes=48 << 20
        ),
        name="mlp_backward",
    )(activations, cotangent, preact, weight, ain, aout, owner)
    return gi, gw.reshape(width, width), li, lo


def solution(mesh):
    placed = (
        P(("dp", "row"), "col"),
        P(("dp", "col"), "row"),
        P(("dp", "col"), "row"),
        P("col", "row"),
        P(None, None, "col"),
        P(None, None, "row"),
        P(),
    )
    return jax.shard_map(
        local,
        mesh=mesh,
        in_specs=placed,
        out_specs=(
            P(("dp", "row"), "col"),
            P("col", "row"),
            P(None, None, "col"),
            P(None, None, "row"),
        ),
        check_vma=False,
    )
```

time: 679 us -> 176 us (0.26)
  the two profiles are of different devices: /device:TPU:6 before, /device:TPU:1 now
where the time goes in v1:
time: 176 us; the launch traced here: 175 us
  Pallas kernels  165 us (94%)
  local copies, waits for them, and re-layouts  9.72 us (6%)
    pallas_call x1, Pallas kernels, local(): pl.pallas_call(kernel, out_shape=(jax.ShapeDtypeStruct((tok, width), BF16...  165 us
    unnamed x18, local copies, waits for them, and re-layouts  9.72 us

profile of v1, /device:TPU:1, one launch (start us, length us, event | category | flops | bytes accessed | tf_op | source)
XLA Modules:
  0.0 175.2 jit_solution(14896422569180676766)
XLA Ops:
  0.6 0.0 copy-start
  0.6 1.3 copy-done
  1.9 0.0 copy-start.1
  1.9 1.0 copy-done.1
  2.9 0.0 copy-start.2
  2.9 1.0 copy-done.2
  3.9 0.0 copy-start.3
  3.9 0.9 copy-done.3
  4.8 0.0 copy-start.4
  4.8 0.9 copy-done.4
  5.7 0.0 copy-start.5
  5.7 0.9 copy-done.5
  6.6 0.0 copy-start.6
  6.6 0.7 copy-done.6
  7.3 164.8 %mlp_backward.1 = (bf16[112,768]{1,0:T(8,128)(2,1)S(1)}, bf16[4,192,768]{2,1,0:T(8,128)(2,1)S(1)}, f32[3,32,768]{2,1,0:T(8,128)S(1)}, f32[3,32,768]{2,1,0:T(8,128)S(1)}) custom-call(bf16[112,768]{1,0:T(8,128)(2,1)S(1)} %copy-done.3, bf16[224,768]{1,0:T(8,128)(2,1)S(1)} %copy-done.1, bf16[224,768]{1,0:T(8,128)(2,1)S(1)} %copy-done.2, ...), custom_call_target="tpu_custom_call" | custom-call | tf_op jit(solution)/shard_map/mlp_backward/pallas_call | solution.py:361
  172.1 0.7 copy.15
  172.8 1.0 copy.16
  173.8 0.7 copy.17
  174.5 0.7 copy.18
Async XLA Ops:
  0.6 1.3 copy-start
  1.9 1.0 copy-start.1
  2.9 1.0 copy-start.2
  3.9 0.9 copy-start.3
  4.8 0.9 copy-start.4
  5.7 0.9 copy-start.5
  6.6 0.7 copy-start.6

commit v2 on v0

v2 whole, which is shorter than its diff:
```python
import functools

import jax
import jax.numpy as jnp
from jax import lax
from jax.experimental import pallas as pl
from jax.experimental.pallas import tpu as pltpu
from jax.sharding import PartitionSpec as P

MESH = pl.DeviceIdType.MESH
F32, BF16 = jnp.float32, jnp.bfloat16
SCALE = 2.0
CUSTOMERS = 3
RANK = 32
LANES = 128


def gelu_slope(v):
    return 0.5 * (1.0 + lax.erf(v * 0.7071067811865476)) + v * jnp.exp(
        -0.5 * v * v
    ) * 0.3989422804014327


def kernel(
    x_in, cot_in, pre_in, w_in, ain_in, aout_in, owner,
    gi_out, gw_out, li_out, lo_out,
    gb, xb, cotv, prev, wv, av, bv, asel, bsel, weff, pb, ra, pa, rx, sz, rza, sza, rzf, giv,
    wb, ry, ow, lgx, lgz, lgt, las, laz, lat, lg, liv, lov,
    load_sem, store_sem, xz_s, xz_r, xx_s, xx_r, g_s, g_r, gk_s, gk_r, ra_s, ra_r, rx_s, rx_r,
    rza_s, rza_r, rzf_s, rzf_r, ry_s, ry_r, ag_s, ag_r, l_s, l_r,
):
    y, r, c = lax.axis_index("dp"), lax.axis_index("row"), lax.axis_index("col")
    i, j, o, k = r // 4, r % 4, c // 2, c % 2
    sign = 1 - 2 * k
    tok = xb.shape[2]
    blk = gb.shape[1]
    width = gb.shape[2]
    wide = width // 2

    def wrap(v):
        return (v + 8) % 4

    def at_x(s):
        return (y, wrap(i + s) * 4 + j, c)

    def at_zhi(s):
        return (y, i * 4 + wrap(j + s), c)

    def at_zlo(s):
        return (y, r, wrap(o + s) * 2 + k)

    def at_y(s):
        return (wrap(y + s), r, c)

    sibling = (y, r, o * 2 + 1 - k)
    ways = (sign, -sign)

    def remote(src, dst, ss, rs, dev):
        return pltpu.make_async_remote_copy(
            src_ref=src, dst_ref=dst, send_sem=ss, recv_sem=rs, device_id=dev, device_id_type=MESH
        )

    halves = [pl.ds(0, wide), pl.ds(wide, wide)]
    loads = [
        pltpu.make_async_copy(a, b, load_sem.at[n])
        for n, (a, b) in enumerate(
            [
                (cot_in, cotv), (pre_in, prev), (w_in, wv), (ain_in, av), (aout_in, bv),
                (x_in.at[:, halves[0]], xb.at[0, r]), (x_in.at[:, halves[1]], xb.at[1, r]),
            ]
        )
    ]
    for cp in loads:
        cp.start()
    barrier = pltpu.get_barrier_semaphore()
    for s in range(1, 4):
        for dev in (at_x(s), at_zhi(s), at_zlo(s), at_y(s)):
            pl.semaphore_signal(barrier, inc=1, device_id=dev, device_id_type=MESH)
    pl.semaphore_signal(barrier, inc=1, device_id=sibling, device_id_type=MESH)

    loads[0].wait()
    loads[1].wait()
    half = blk // 2
    for h in range(2):
        rows = pl.ds(h * half, half)
        v = prev[rows, :].astype(F32)
        gb[c, rows, :] = (cotv[rows, :].astype(F32) * gelu_slope(v)).astype(BF16)
    loads[3].wait()
    loads[4].wait()
    mine = owner[y]
    a_sum = jnp.zeros(asel.shape, F32)
    b_sum = jnp.zeros(bsel.shape, F32)
    for n in range(CUSTOMERS):
        a_sum = a_sum + jnp.where(mine == n, av[n].astype(F32), 0.0)
        b_sum = b_sum + jnp.where(mine == n, bv[n].astype(F32), 0.0)
    asel[...] = a_sum.astype(BF16)
    bsel[...] = b_sum.astype(BF16)
    loads[2].wait()
    fold = lax.dot_general(asel[...], bsel[...], (((0,), (0,)), ((), ())), preferred_element_type=F32)
    weff[...] = (wv[...].astype(F32) + SCALE * fold).astype(BF16)

    def nt(a, b):
        return lax.dot_general(a, b, (((1,), (1,)), ((), ())), preferred_element_type=F32)

    lgx[i] = jnp.zeros(lgx.shape[1:], BF16)
    for h in range(2):
        lgx[i, :, h * LANES : h * LANES + half] = nt(bsel[...], gb[c, h * half : (h + 1) * half, :]).astype(BF16)
    loads[5].wait()
    loads[6].wait()
    las[k] = jnp.zeros(las.shape[1:], BF16)
    las[k, :, :tok] = (nt(asel[:, :wide], xb[0, r]) + nt(asel[:, wide:], xb[1, r])).astype(BF16)

    def lgx_send(s):
        return remote(lgx.at[i], lgx.at[i], l_s.at[0, s - 1], l_r.at[0, s - 1], at_x(s))

    def las_send():
        return remote(las.at[k], las.at[k], l_s.at[1, 0], l_r.at[1, 0], sibling)

    def lgz_send(s):
        return remote(lgz.at[j], lgz.at[j], l_s.at[2, s - 1], l_r.at[2, s - 1], at_zhi(s))

    def laz_send(s):
        return remote(laz.at[o], laz.at[o], l_s.at[3, s - 1], l_r.at[3, s - 1], at_zlo(s))

    def lgt_send(s):
        return remote(lgt.at[k, o], lgt.at[k, o], l_s.at[4, s - 1], l_r.at[4, s - 1], at_zlo(s))

    def lat_send(s):
        return remote(lat.at[i, j], lat.at[i, j], l_s.at[5, s - 1], l_r.at[5, s - 1], at_zhi(s))

    def lgt_sib():
        return remote(lgt.at[k], lgt.at[k], l_s.at[6, 0], l_r.at[6, 0], sibling)

    def lat_x(s):
        return remote(lat.at[i], lat.at[i], l_s.at[7, s - 1], l_r.at[7, s - 1], at_x(s))

    def lg_y(s):
        return remote(lg.at[y], lg.at[y], l_s.at[8, s - 1], l_r.at[8, s - 1], at_y(s))

    def xz_own(h, e):
        return remote(xb.at[h, r], xb.at[h, r], xz_s.at[h, e], xz_r.at[h, e], at_zhi(ways[e]))

    def xz_on(h):
        row = i * 4 + wrap(j - ways[h])
        return remote(xb.at[h, row], xb.at[h, row], xz_s.at[h, 2], xz_r.at[h, 2], at_zhi(ways[h]))

    def xrow(ii, q):
        return wrap(ii) * 4 + wrap(j + (0, -sign, sign, 2)[q])

    def xx_own(q, h, e):
        row = xrow(i, q)
        return remote(xb.at[h, row], xb.at[h, row], xx_s.at[q, h, e], xx_r.at[q, h, e], at_x(ways[e]))

    def xx_on(q, h):
        row = xrow(i - ways[h], q)
        return remote(xb.at[h, row], xb.at[h, row], xx_s.at[q, h, 2], xx_r.at[q, h, 2], at_x(ways[h]))

    def xx_start(q, h):
        for e in range(2):
            xx_own(q, h, e).start()

    def xx_forward(q, h):
        xx_own(q, h, h).wait_recv()
        xx_on(q, h).start()

    def g_hop(d, s):
        oo = wrap(o - s) if d == 0 else wrap(o + s)
        b = oo * 2 + k
        return remote(gb.at[b], gb.at[b], g_s.at[d, s], g_r.at[d, s], at_zlo(1 - 2 * d))

    def g_sib(d, s):
        oo = wrap(o - s) if d == 0 else wrap(o + s)
        b = oo * 2 + k
        return remote(gb.at[b], gb.at[b], gk_s.at[d, s], gk_r.at[d, s], sibling)

    def ra_send(kk):
        return remote(
            pb.at[wrap(i + 2) * 2 + kk], ra.at[kk], ra_s.at[kk], ra_r.at[kk], at_x(sign * (1 - 2 * kk))
        )

    def rx_send(kk):
        way = sign * (2 * kk - 1)
        return remote(
            pb.at[wrap(i + way) * 2 + kk], rx.at[1 - kk, kk], rx_s.at[1 - kk, kk], rx_r.at[1 - kk, kk], at_x(way)
        )

    def pa_send(kk):
        return remote(pa.at[kk], rx.at[kk, kk], rx_s.at[kk, kk], rx_r.at[kk, kk], at_x(ways[kk]))

    def part(oo, kk):
        b = oo * 2 + kk
        pb[b] = nt(gb[b], weff[...]).astype(BF16)

    def part_send(oo, kk):
        rel = wrap((oo - i) * sign)

        @pl.when(rel == 2)
        def _():
            ra_send(kk).start()

        @pl.when(rel == 3 - 2 * kk)
        def _():
            rx_send(kk).start()

    part(o, k)

    with jax.named_scope("entry"):
        pl.semaphore_wait(barrier, 13)

    with jax.named_scope("first sends"):
        for s in range(1, 4):
            lgx_send(s).start()
        las_send().start()

        @pl.when(o < 3)
        def _():
            g_hop(0, 0).start()

        @pl.when(o > 0)
        def _():
            g_hop(1, 0).start()

        g_sib(0, 0).start()
        part_send(o, k)
        for e in range(2):
            xz_own(0, e).start()
        for h in range(2):
            xx_start(0, h)
    with jax.named_scope("own block"):
        g_sib(0, 0).wait_recv()
        part(o, 1 - k)
        part_send(o, 1 - k)

    for s in range(1, 4):
        lgx_send(s).wait_recv()

    def sum4(ref):
        return (ref[0].astype(F32) + ref[1].astype(F32)) + (ref[2].astype(F32) + ref[3].astype(F32))

    with jax.named_scope("rank stage 2"):
        lgz[j] = sum4(lgx).astype(BF16)
        las_send().wait_recv()
        laz[o] = (las[0].astype(F32) + las[1].astype(F32)).astype(BF16)
        for s in range(1, 4):
            lgz_send(s).start()
            laz_send(s).start()
    def g_step(s):
        for d in range(2):
            here = (o >= s) if d == 0 else (o <= 3 - s)
            oo = wrap(o - s) if d == 0 else wrap(o + s)

            @pl.when(here)
            def _():
                g_hop(d, s - 1).wait_recv()

            @pl.when(jnp.logical_and(here, (o < 3) if d == 0 else (o > 0)))
            def _():
                g_hop(d, s).start()

            @pl.when(here)
            def _():
                g_sib(d, s).start()
                part(oo, k)
                part_send(oo, k)

        for d in range(2):
            here = (o >= s) if d == 0 else (o <= 3 - s)
            oo = wrap(o - s) if d == 0 else wrap(o + s)

            @pl.when(here)
            def _():
                g_sib(d, s).wait_recv()
                part(oo, 1 - k)
                part_send(oo, 1 - k)

    with jax.named_scope("gradients 1"):
        g_step(1)
    for e in range(2):
        xz_own(1, e).start()
    with jax.named_scope("act x own"):
        for h in range(2):
            xx_forward(0, h)
    with jax.named_scope("act z own 0"):
        for e in range(2):
            xz_own(0, e).wait_recv()
        xz_on(0).start()
        xx_start(1, 0)
        xx_start(2, 0)

    with jax.named_scope("gradients 2"):
        g_step(2)

    with jax.named_scope("rank stage 3"):
        for s in range(1, 4):
            lgz_send(s).wait_recv()
            laz_send(s).wait_recv()
        lgt[k, o] = sum4(lgz).astype(BF16)
        lat[i, j] = sum4(laz).astype(BF16)
        for s in range(1, 4):
            lgt_send(s).start()
            lat_send(s).start()
    with jax.named_scope("act z own 1"):
        for e in range(2):
            xz_own(1, e).wait_recv()
        xz_on(1).start()
        xx_start(1, 1)
        xx_start(2, 1)
    with jax.named_scope("act x on 0"):
        xx_forward(1, 0)
        xx_forward(2, 0)

    with jax.named_scope("gradients 3"):
        g_step(3)

    with jax.named_scope("input sums x"):
        for kk in range(2):
            ra_send(kk).wait_recv()
            b = wrap(i + ways[kk]) * 2 + kk
            pa[kk] = (pb[b].astype(F32) + ra[kk].astype(F32)).astype(BF16)
            pa_send(kk).start()
    with jax.named_scope("act z on 0"):
        xz_on(0).wait_recv()
        xx_start(3, 0)
    with jax.named_scope("act x on 1"):
        xx_forward(1, 1)
        xx_forward(2, 1)
    with jax.named_scope("act z on 1"):
        xz_on(1).wait_recv()
        xx_start(3, 1)
    with jax.named_scope("act x last"):
        xx_forward(3, 0)
        xx_forward(3, 1)

    with jax.named_scope("rank stage 4"):
        for s in range(1, 4):
            lgt_send(s).wait_recv()
            lat_send(s).wait_recv()
        lgt_sib().start()
        for s in range(1, 4):
            lat_x(s).start()
    def ry_send(h, s):
        return remote(wb.at[h, wrap(y + s)], ry.at[h, s - 1], ry_s.at[h, s - 1], ry_r.at[h, s - 1], at_y(s))

    gs = gb[...].reshape(8 * blk, width)

    def product(h):
        with jax.named_scope("product waits"):
            for q in range(4):
                xx_own(q, h, 1 - h).wait_recv()
                xx_on(q, h).wait_recv()
        term = lax.dot_general(
            xb[h].reshape(16 * tok, wide), gs, (((0,), (0,)), ((), ())), preferred_element_type=F32
        )
        wb[h] = term.astype(BF16).reshape(wb.shape[1:])
        for s in range(1, 4):
            ry_send(h, s).start()

    with jax.named_scope("product 0"):
        product(0)

    with jax.named_scope("input wait x"):
        for kk in range(2):
            pa_send(kk).wait_recv()
            rx_send(kk).wait_recv()
    for q in range(4):
        kk, rows = q // 2, pl.ds((q % 2) * tok, tok)
        total = pb[i * 2 + kk, rows, :].astype(F32)
        for e in range(2):
            total = total + rx[e, kk, rows, :].astype(F32)
        total = total.astype(BF16)
        sz[q, 0] = total[:, :wide]
        sz[q, 1] = total[:, wide:]

    def rza_send(h):
        return remote(sz.at[wrap(j + 2), h], rza.at[h], rza_s.at[h], rza_r.at[h], at_zhi(ways[h]))

    def rzf_send(h):
        way = ways[1 - h]
        return remote(
            sz.at[wrap(j + way), h], rzf.at[1 - h, h], rzf_s.at[1 - h, h], rzf_r.at[1 - h, h], at_zhi(way)
        )

    def sza_send(h):
        return remote(sza.at[h], rzf.at[h, h], rzf_s.at[h, h], rzf_r.at[h, h], at_zhi(ways[h]))

    for h in range(2):
        rza_send(h).start()
    for h in range(2):
        rzf_send(h).start()

    with jax.named_scope("product 1"):
        product(1)

    with jax.named_scope("adapters"):
        lgt_sib().wait_recv()
        for s in range(1, 4):
            lat_x(s).wait_recv()
        lout = jnp.zeros((RANK, width), F32)
        lin = [jnp.zeros((RANK, wide), F32), jnp.zeros((RANK, wide), F32)]
        for b in range(8):
            for p in range(2):
                row = 2 * b + p
                lout = lout + jnp.dot(
                    lat[row // 4, row % 4, :, :tok], gb[b, p * tok : (p + 1) * tok, :], preferred_element_type=F32
                )
                low = lgt[b % 2, b // 2, :, p * LANES : p * LANES + tok]
                for h in range(2):
                    lin[h] = lin[h] + jnp.dot(low, xb[h, row], preferred_element_type=F32)
        for h in range(2):
            lg[y, :RANK, h * wide : (h + 1) * wide] = (SCALE * lin[h]).astype(BF16)
        lg[y, RANK:] = (SCALE * lout).astype(BF16)
        for s in range(1, 4):
            lg_y(s).start()
    def ow_ag(h, s):
        return remote(ow.at[h, y], ow.at[h, y], ag_s.at[h, s - 1], ag_r.at[h, s - 1], at_y(s))

    def sum_y(h):
        for s in range(1, 4):
            ry_send(h, s).wait_recv()
        total = wb[h, y].astype(F32)
        for s in range(3):
            total = total + ry[h, s].astype(F32)
        ow[h, y] = total.astype(BF16)
        for s in range(1, 4):
            ow_ag(h, s).start()

    with jax.named_scope("y sum 0"):
        sum_y(0)
    with jax.named_scope("input sums z"):
        for h in range(2):
            rza_send(h).wait_recv()
            sza[h] = (sz[wrap(j + ways[h]), h].astype(F32) + rza[h].astype(F32)).astype(BF16)
            sza_send(h).start()
    with jax.named_scope("y sum 1"):
        sum_y(1)

    with jax.named_scope("adapters wait y"):
        for s in range(1, 4):
            lg_y(s).wait_recv()
    for n in range(CUSTOMERS):
        acc = jnp.zeros((2 * RANK, width), F32)
        for g in range(4):
            acc = acc + jnp.where(owner[g] == n, lg[g].astype(F32), 0.0)
        liv[n] = acc[:RANK]
        lov[n] = acc[RANK:]
    li_store = pltpu.make_async_copy(liv, li_out, store_sem.at[1])
    lo_store = pltpu.make_async_copy(lov, lo_out, store_sem.at[2])
    li_store.start()
    lo_store.start()
    with jax.named_scope("input wait z"):
        for h in range(2):
            rzf_send(h).wait_recv()
            sza_send(h).wait_recv()
    for h in range(2):
        total = sz[j, h].astype(F32)
        for e in range(2):
            total = total + rzf[e, h].astype(F32)
        giv[:, h * wide : (h + 1) * wide] = total.astype(BF16)
    gi_store = pltpu.make_async_copy(giv, gi_out, store_sem.at[0])
    gi_store.start()
    with jax.named_scope("y gather"):
        gw_stores = []
        for h in range(2):
            for s in range(1, 4):
                ow_ag(h, s).wait_recv()
            gw_stores.append(pltpu.make_async_copy(ow.at[h], gw_out.at[h], store_sem.at[3 + h]))
            gw_stores[h].start()
    with jax.named_scope("sent"):
        for d in range(2):
            for s in range(3):
                sent = (o >= s) if d == 0 else (o <= 3 - s)

                @pl.when(jnp.logical_and(sent, (o < 3) if d == 0 else (o > 0)))
                def _():
                    g_hop(d, s).wait_send()

                if s > 0 or d == 0:

                    @pl.when(sent)
                    def _():
                        g_sib(d, s).wait_send()

            @pl.when((o == 3) if d == 0 else (o == 0))
            def _():
                g_sib(d, 3).wait_send()

        for h in range(2):
            for e in range(2):
                xz_own(h, e).wait_send()
            xz_on(h).wait_send()
            for q in range(4):
                for e in range(2):
                    xx_own(q, h, e).wait_send()
                xx_on(q, h).wait_send()
            ra_send(h).wait_send()
            rx_send(h).wait_send()
            pa_send(h).wait_send()
            rza_send(h).wait_send()
            rzf_send(h).wait_send()
            sza_send(h).wait_send()
            for s in range(1, 4):
                ry_send(h, s).wait_send()
                ow_ag(h, s).wait_send()
        las_send().wait_send()
        lgt_sib().wait_send()
        for s in range(1, 4):
            for small in (lgx_send, lgz_send, laz_send, lgt_send, lat_send, lat_x, lg_y):
                small(s).wait_send()
    for cp in [gi_store, li_store, lo_store, *gw_stores]:
        cp.wait()


def local(activations, cotangent, preact, weight, ain, aout, owner):
    tok, width = activations.shape
    blk = cotangent.shape[0]
    wide = width // 2
    eighth = width // 8
    hbm = pl.BlockSpec(memory_space=pltpu.HBM)
    dma = pltpu.SemaphoreType.DMA
    v = pltpu.VMEM
    scratch = [
        v((8, blk, width), BF16),
        v((2, 16, tok, wide), BF16),
        v((blk, width), BF16),
        v((blk, width), BF16),
        v((width, width), BF16),
        v((CUSTOMERS, RANK, width), BF16),
        v((CUSTOMERS, RANK, width), BF16),
        v((RANK, width), BF16),
        v((RANK, width), BF16),
        v((width, width), BF16),
        v((8, blk, width), BF16),
        v((2, blk, width), BF16),
        v((2, blk, width), BF16),
        v((2, 2, blk, width), BF16),
        v((4, 2, tok, wide), BF16),
        v((2, tok, wide), BF16),
        v((2, tok, wide), BF16),
        v((2, 2, tok, wide), BF16),
        v((tok, width), BF16),
        v((2, 4, eighth, width), BF16),
        v((2, 3, eighth, width), BF16),
        v((2, 4, eighth, width), BF16),
        v((4, RANK, 2 * LANES), BF16),
        v((4, RANK, 2 * LANES), BF16),
        v((2, 4, RANK, 2 * LANES), BF16),
        v((2, RANK, LANES), BF16),
        v((4, RANK, LANES), BF16),
        v((4, 4, RANK, LANES), BF16),
        v((4, 2 * RANK, width), BF16),
        v((CUSTOMERS, RANK, width), F32),
        v((CUSTOMERS, RANK, width), F32),
        dma((7,)), dma((5,)),
        dma((2, 3)), dma((2, 3)), dma((4, 2, 3)), dma((4, 2, 3)),
        dma((2, 4)), dma((2, 4)), dma((2, 4)), dma((2, 4)),
        dma((2,)), dma((2,)), dma((2, 2)), dma((2, 2)),
        dma((2,)), dma((2,)), dma((2, 2)), dma((2, 2)),
        dma((2, 3)), dma((2, 3)), dma((2, 3)), dma((2, 3)),
        dma((9, 3)), dma((9, 3)),
    ]
    gi, gw, li, lo = pl.pallas_call(
        kernel,
        out_shape=(
            jax.ShapeDtypeStruct((tok, width), BF16),
            jax.ShapeDtypeStruct((2, 4, eighth, width), BF16),
            jax.ShapeDtypeStruct((CUSTOMERS, RANK, width), F32),
            jax.ShapeDtypeStruct((CUSTOMERS, RANK, width), F32),
        ),
        in_specs=[hbm] * 6 + [pl.BlockSpec(memory_space=pltpu.SMEM)],
        out_specs=[hbm] * 4,
        scratch_shapes=scratch,
        compiler_params=pltpu.CompilerParams(
            collective_id=0, has_side_effects=True, vmem_limit_bytes=60 << 20
        ),
        name="mlp_backward",
    )(activations, cotangent, preact, weight, ain, aout, owner)
    return gi, gw.reshape(width, width), li, lo


def solution(mesh):
    placed = (
        P(("dp", "row"), "col"),
        P(("dp", "col"), "row"),
        P(("dp", "col"), "row"),
        P("col", "row"),
        P(None, None, "col"),
        P(None, None, "row"),
        P(),
    )
    return jax.shard_map(
        local,
        mesh=mesh,
        in_specs=placed,
        out_specs=(
            P(("dp", "row"), "col"),
            P("col", "row"),
            P(None, None, "col"),
            P(None, None, "row"),
        ),
        check_vma=False,
    )
```

time: 679 us -> 136 us (0.20)
  waiting for transfers between devices: 625 us -> 0 us
  Pallas kernels: 0 us -> 129 us
  matrix products: 26 us -> 0 us
  between operations: 16.1 us -> 0.64 us
    psum x3 -> x0, waiting for transfers between devices: 322 us -> none  [the longest x1 189 us: local(): rank_gradient = lax.psum(rank_everything.astype(jnp.bfloat16), 'row')]
    all_gather x2 -> x0, waiting for transfers between devices: 155 us -> none  [the longest x1 107 us: local(): every_activation = lax.all_gather(activations, 'row', axis=0, tiled=True)]
    reduce_scatter x1 -> x0, waiting for transfers between devices: 147 us -> none  [local(): lax.psum_scatter((incomplete_term + adapter_scale_factor * jnp.dot(rank_e...]
    pallas_call x0 -> x1, Pallas kernels: none -> 129 us  [local(): pl.pallas_call(kernel, out_shape=(jax.ShapeDtypeStruct((tok, width), BF16...]
    dot_general x7 -> x0, matrix products: 26 us -> none  [the longest x1 5.99 us: local(): lax.dot_general(every_activation, every_gradient, (((0,), (0,)), ((), ())...]
  transfers between devices with their start and end apart: 6 -> 0, of which waited for: 6 -> 0; matrix products, arithmetic and copies ran while one was open for 4% -> 0% of each run, Pallas kernels for 0% -> 0%
where the time goes in v2:
time: 136 us; the launch traced here: 135 us
  Pallas kernels  129 us (95%)
  local copies, waits for them, and re-layouts  5.45 us (4%)
    pallas_call x1, Pallas kernels, local(): pl.pallas_call(kernel, out_shape=(jax.ShapeDtypeStruct((tok, width), BF16...  129 us
    unnamed x8, local copies, waits for them, and re-layouts  5.45 us

profile of v2, /device:TPU:6, one launch (start us, length us, event | category | flops | bytes accessed | tf_op | source)
XLA Modules:
  0.0 135.4 jit_solution(4449821563093151800)
XLA Ops:
  0.6 129.3 %mlp_backward.1 = (bf16[112,768]{1,0:T(8,128)(2,1)}, bf16[2,4,96,768]{3,2,1,0:T(8,128)(2,1)}, f32[3,32,768]{2,1,0:T(8,128)}, f32[3,32,768]{2,1,0:T(8,128)}) custom-call(bf16[112,768]{1,0:T(8,128)(2,1)} %x_in.1, bf16[224,768]{1,0:T(8,128)(2,1)} %cot_in.1, bf16[224,768]{1,0:T(8,128)(2,1)} %pre_in.1, bf16[768,768]{1,0:T(8,128)(2,1)} %w_in.1, ...), custom_call_target="tpu_custom_call" | custom-call | tf_op jit(solution)/shard_map/mlp_backward/pallas_call | solution.py:561
  129.9 1.6 %copy.15 = bf16[112,768]{1,0:T(8,128)(2,1)} copy(bf16[112,768]{1,0:T(8,128)(2,1)} %get-tuple-element.16) | data formatting | bytes 344064
  131.5 0.0 copy-start.1
  131.5 0.0 copy-start
  131.5 2.4 %copy.16 = bf16[768,768]{1,0:T(8,128)(2,1)} copy(bf16[768,768]{1,0:T(8,128)(2,1)} %bitcast.1) | data formatting | bytes 2359296
  133.9 0.0 copy-done.1
  133.9 0.7 copy.17
  134.7 0.0 copy-done
  134.7 0.7 copy.18
Async XLA Ops:
  131.5 2.4 %copy-start.1 = (f32[3,32,768]{2,1,0:T(8,128)S(1)}, f32[3,32,768]{2,1,0:T(8,128)}, u32[]{:S(2)}) copy-start(f32[3,32,768]{2,1,0:T(8,128)} %get-tuple-element.18) | copy-start | bytes 884740
  131.5 3.1 %copy-start = (f32[3,32,768]{2,1,0:T(8,128)S(1)}, f32[3,32,768]{2,1,0:T(8,128)}, u32[]{:S(2)}) copy-start(f32[3,32,768]{2,1,0:T(8,128)} %get-tuple-element.19) | copy-start | bytes 884740

commit v3 on v2

v3 whole, which is shorter than its diff:
```python
import functools

import jax
import jax.numpy as jnp
from jax import lax
from jax.experimental import pallas as pl
from jax.experimental.pallas import tpu as pltpu
from jax.sharding import PartitionSpec as P

MESH = pl.DeviceIdType.MESH
F32, BF16 = jnp.float32, jnp.bfloat16
SCALE = 2.0
CUSTOMERS = 3
RANK = 32
LANES = 128
PARTS = 3


def gelu_slope(v):
    return 0.5 * (1.0 + lax.erf(v * 0.7071067811865476)) + v * jnp.exp(
        -0.5 * v * v
    ) * 0.3989422804014327


def kernel(
    x_in, cot_in, pre_in, w_in, ain_in, aout_in, owner,
    gi_out, gw_out, li_out, lo_out,
    gb, xb, cotv, prev, wv, av, bv, asel, bsel, weff, pb, ra, pa, rx, sz, rza, sza, rzf,
    wb, ryo, ryp, ryf, lgx, lgz, lgt, las, laz, lat, lg,
    load_sem, xz_s, xz_r, xx_s, xx_r, g_s, g_r, gk_s, gk_r, ra_s, ra_r, rx_s, rx_r,
    rza_s, rza_r, rzf_s, rzf_r, yo_s, yo_r, yd_s, yd_r, yp_s, yp_r, ag_s, ag_r, l_s, l_r,
):
    y, r, c = lax.axis_index("dp"), lax.axis_index("row"), lax.axis_index("col")
    i, j, o, k = r // 4, r % 4, c // 2, c % 2
    sign = 1 - 2 * k
    tok = xb.shape[2]
    blk = gb.shape[1]
    half = blk // 2
    width = gb.shape[2]
    wide = width // 2
    third = width // PARTS

    def wrap(v):
        return (v + 8) % 4

    def at_x(s):
        return (y, wrap(i + s) * 4 + j, c)

    def at_zhi(s):
        return (y, i * 4 + wrap(j + s), c)

    def at_zlo(s):
        return (y, r, wrap(o + s) * 2 + k)

    def at_y(s):
        return (wrap(y + s), r, c)

    sibling = (y, r, o * 2 + 1 - k)
    ways = (sign, -sign)

    def remote(src, dst, ss, rs, dev):
        return pltpu.make_async_remote_copy(
            src_ref=src, dst_ref=dst, send_sem=ss, recv_sem=rs, device_id=dev, device_id_type=MESH
        )

    loads = [
        pltpu.make_async_copy(a, b, load_sem.at[n])
        for n, (a, b) in enumerate(
            [(cot_in, cotv), (pre_in, prev), (w_in, wv), (ain_in, av), (aout_in, bv)]
            + [(x_in.at[:, pl.ds(t * third, third)], xb.at[t, r]) for t in range(PARTS)]
        )
    ]
    for cp in loads:
        cp.start()
    barrier = pltpu.get_barrier_semaphore()
    for s in range(1, 4):
        for dev in (at_x(s), at_zhi(s), at_zlo(s), at_y(s)):
            pl.semaphore_signal(barrier, inc=1, device_id=dev, device_id_type=MESH)
    pl.semaphore_signal(barrier, inc=1, device_id=sibling, device_id_type=MESH)

    def nt(a, b):
        return lax.dot_general(a, b, (((1,), (1,)), ((), ())), preferred_element_type=F32)

    def lgx_send(s):
        return remote(lgx.at[i], lgx.at[i], l_s.at[0, s - 1], l_r.at[0, s - 1], at_x(s))

    def las_send():
        return remote(las.at[k], las.at[k], l_s.at[1, 0], l_r.at[1, 0], sibling)

    def lgz_send(s):
        return remote(lgz.at[j], lgz.at[j], l_s.at[2, s - 1], l_r.at[2, s - 1], at_zhi(s))

    def laz_send(s):
        return remote(laz.at[o], laz.at[o], l_s.at[3, s - 1], l_r.at[3, s - 1], at_zlo(s))

    def lgt_send(s):
        return remote(lgt.at[k, o], lgt.at[k, o], l_s.at[4, s - 1], l_r.at[4, s - 1], at_zlo(s))

    def lat_send(s):
        return remote(lat.at[i, j], lat.at[i, j], l_s.at[5, s - 1], l_r.at[5, s - 1], at_zhi(s))

    def lgt_sib():
        return remote(lgt.at[k], lgt.at[k], l_s.at[6, 0], l_r.at[6, 0], sibling)

    def lat_x(s):
        return remote(lat.at[i], lat.at[i], l_s.at[7, s - 1], l_r.at[7, s - 1], at_x(s))

    def lg_y(n, s):
        return remote(lg.at[n, y], lg.at[n, y], l_s.at[8 + n, s - 1], l_r.at[8 + n, s - 1], at_y(s))

    def xz_own(h, e):
        return remote(xb.at[h, r], xb.at[h, r], xz_s.at[h, e], xz_r.at[h, e], at_zhi(ways[e]))

    def xz_on(h):
        way = ways[h % 2]
        row = i * 4 + wrap(j - way)
        return remote(xb.at[h, row], xb.at[h, row], xz_s.at[h, 2], xz_r.at[h, 2], at_zhi(way))

    def xrow(ii, q):
        return wrap(ii) * 4 + wrap(j + (0, -sign, sign, 2)[q])

    def xx_own(q, h, e):
        row = xrow(i, q)
        return remote(xb.at[h, row], xb.at[h, row], xx_s.at[q, h, e], xx_r.at[q, h, e], at_x(ways[e]))

    def xx_on(q, h):
        way = ways[h % 2]
        row = xrow(i - way, q)
        return remote(xb.at[h, row], xb.at[h, row], xx_s.at[q, h, 2], xx_r.at[q, h, 2], at_x(way))

    def xx_start(q, h):
        for e in range(2):
            xx_own(q, h, e).start()

    def xx_forward(q, h):
        xx_own(q, h, h % 2).wait_recv()
        xx_on(q, h).start()

    def g_block(d, s):
        return (wrap(o - s) if d == 0 else wrap(o + s)) * 2 + k

    def g_hop(d, s, h):
        ref = gb.at[g_block(d, s), pl.ds(h * half, half)]
        return remote(ref, ref, g_s.at[d, s, h], g_r.at[d, s, h], at_zlo(1 - 2 * d))

    def g_sib(d, s, h):
        ref = gb.at[g_block(d, s), pl.ds(h * half, half)]
        return remote(ref, ref, gk_s.at[d, s, h], gk_r.at[d, s, h], sibling)

    def ra_send(kk):
        return remote(
            pb.at[wrap(i + 2) * 2 + kk], ra.at[kk], ra_s.at[kk], ra_r.at[kk], at_x(sign * (1 - 2 * kk))
        )

    def rx_send(kk):
        way = sign * (2 * kk - 1)
        return remote(
            pb.at[wrap(i + way) * 2 + kk], rx.at[1 - kk, kk], rx_s.at[1 - kk, kk], rx_r.at[1 - kk, kk], at_x(way)
        )

    def pa_send(kk):
        return remote(pa.at[kk], rx.at[kk, kk], rx_s.at[kk, kk], rx_r.at[kk, kk], at_x(ways[kk]))

    def part(oo, kk):
        b = oo * 2 + kk
        pb[b] = nt(gb[b], weff[...]).astype(BF16)

    def part_send(oo, kk):
        rel = wrap((oo - i) * sign)

        @pl.when(rel == 2)
        def _():
            ra_send(kk).start()

        @pl.when(rel == 3 - 2 * kk)
        def _():
            rx_send(kk).start()

    loads[0].wait()
    loads[1].wait()
    for h in range(2):
        rows = pl.ds(h * half, half)
        v = prev[rows, :].astype(F32)
        gb[c, rows, :] = (cotv[rows, :].astype(F32) * gelu_slope(v)).astype(BF16)
    for t in range(PARTS):
        loads[5 + t].wait()
    with jax.named_scope("entry"):
        pl.semaphore_wait(barrier, 13)

    for h in range(2):

        @pl.when(o < 3)
        def _():
            g_hop(0, 0, h).start()

        @pl.when(o > 0)
        def _():
            g_hop(1, 0, h).start()

    for h in range(2):
        g_sib(0, 0, h).start()

    with jax.named_scope("fold"):
        loads[3].wait()
        loads[4].wait()
        mine = owner[y]
        a_sum = jnp.zeros(asel.shape, F32)
        b_sum = jnp.zeros(bsel.shape, F32)
        for n in range(CUSTOMERS):
            a_sum = a_sum + jnp.where(mine == n, av[n].astype(F32), 0.0)
            b_sum = b_sum + jnp.where(mine == n, bv[n].astype(F32), 0.0)
        asel[...] = a_sum.astype(BF16)
        bsel[...] = b_sum.astype(BF16)
        loads[2].wait()
        fold = lax.dot_general(
            asel[...], bsel[...], (((0,), (0,)), ((), ())), preferred_element_type=F32
        )
        weff[...] = (wv[...].astype(F32) + SCALE * fold).astype(BF16)

    with jax.named_scope("rank stage 1"):
        lgx[i] = jnp.zeros(lgx.shape[1:], BF16)
        for h in range(2):
            lgx[i, :, h * LANES : h * LANES + half] = nt(
                bsel[...], gb[c, h * half : (h + 1) * half, :]
            ).astype(BF16)
        las[k] = jnp.zeros(las.shape[1:], BF16)
        low = jnp.zeros((RANK, tok), F32)
        for t in range(PARTS):
            low = low + nt(asel[:, t * third : (t + 1) * third], xb[t, r])
        las[k, :, :tok] = low.astype(BF16)
        for s in range(1, 4):
            lgx_send(s).start()
        las_send().start()

    with jax.named_scope("own block"):
        part(o, k)
        part_send(o, k)
        for h in range(2):
            g_sib(0, 0, h).wait_recv()
        part(o, 1 - k)
        part_send(o, 1 - k)
        for t in range(PARTS):
            xx_start(0, t)

    def sum4(ref):
        return (ref[0].astype(F32) + ref[1].astype(F32)) + (ref[2].astype(F32) + ref[3].astype(F32))

    def g_step(s):
        for d in range(2):
            here = (o >= s) if d == 0 else (o <= 3 - s)
            oo = wrap(o - s) if d == 0 else wrap(o + s)
            for h in range(2):

                @pl.when(here)
                def _():
                    g_hop(d, s - 1, h).wait_recv()

                @pl.when(jnp.logical_and(here, (o < 3) if d == 0 else (o > 0)))
                def _():
                    g_hop(d, s, h).start()

                @pl.when(here)
                def _():
                    g_sib(d, s, h).start()

            @pl.when(here)
            def _():
                part(oo, k)
                part_send(oo, k)

        for d in range(2):
            here = (o >= s) if d == 0 else (o <= 3 - s)
            oo = wrap(o - s) if d == 0 else wrap(o + s)

            @pl.when(here)
            def _():
                for h in range(2):
                    g_sib(d, s, h).wait_recv()
                part(oo, 1 - k)
                part_send(oo, 1 - k)

    def pass_on(dist):
        with jax.named_scope(f"input sums x {dist}"):
            for kk in range(2):
                ii = wrap(i + ways[kk])

                @pl.when(jnp.logical_or(o - ii == dist, ii - o == dist))
                def _():
                    ra_send(kk).wait_recv()
                    pa[kk] = (pb[ii * 2 + kk].astype(F32) + ra[kk].astype(F32)).astype(BF16)
                    pa_send(kk).start()

    def act_z(t):
        with jax.named_scope(f"act z {t}"):
            for e in range(2):
                xz_own(t, e).wait_recv()
            xz_on(t).start()
            xx_start(1, t)
            xx_start(2, t)

    def act_z_last(t):
        with jax.named_scope(f"act z last {t}"):
            xz_on(t).wait_recv()
            xx_start(3, t)

    def act_x(q, t):
        with jax.named_scope(f"act x {q} {t}"):
            xx_forward(q, t)

    def xz_start(t):
        for e in range(2):
            xz_own(t, e).start()

    with jax.named_scope("gradients 1"):
        g_step(1)
    pass_on(0)
    for t in range(PARTS):
        act_x(0, t)
    with jax.named_scope("gradients 2"):
        g_step(2)
    xz_start(0)
    pass_on(1)
    with jax.named_scope("rank stage 2"):
        for s in range(1, 4):
            lgx_send(s).wait_recv()
        lgz[j] = sum4(lgx).astype(BF16)
        las_send().wait_recv()
        laz[o] = (las[0].astype(F32) + las[1].astype(F32)).astype(BF16)
        for s in range(1, 4):
            lgz_send(s).start()
            laz_send(s).start()
    with jax.named_scope("gradients 3"):
        g_step(3)
    xz_start(1)
    pass_on(2)
    act_z(0)
    with jax.named_scope("rank stage 3"):
        for s in range(1, 4):
            lgz_send(s).wait_recv()
            laz_send(s).wait_recv()
        lgt[k, o] = sum4(lgz).astype(BF16)
        lat[i, j] = sum4(laz).astype(BF16)
        for s in range(1, 4):
            lgt_send(s).start()
            lat_send(s).start()
    xz_start(2)
    act_x(1, 0)
    act_x(2, 0)
    act_z_last(0)
    act_z(1)
    pass_on(3)
    act_x(3, 0)
    act_x(1, 1)
    act_x(2, 1)
    act_z(2)
    act_z_last(1)
    with jax.named_scope("rank stage 4"):
        for s in range(1, 4):
            lgt_send(s).wait_recv()
            lat_send(s).wait_recv()
        lgt_sib().start()
        for s in range(1, 4):
            lat_x(s).start()
    low_rows = wb.shape[2] // 2
    cuts = (pl.ds(0, low_rows), pl.ds(low_rows, low_rows))

    def yo_send(t, e):
        return remote(
            wb.at[t, wrap(y + 2), cuts[e]], ryo.at[t, e], yo_s.at[t, e], yo_r.at[t, e], at_y(ways[e])
        )

    def yd_send(t, e):
        return remote(
            wb.at[t, wrap(y + ways[e]), cuts[1 - e]], ryf.at[t, e, 1 - e], yd_s.at[t, e], yd_r.at[t, e], at_y(ways[e])
        )

    def yp_send(t, e):
        return remote(ryp.at[t, e], ryf.at[t, e, e], yp_s.at[t, e], yp_r.at[t, e], at_y(ways[e]))

    def pass_y(t):
        with jax.named_scope(f"y pass {t}"):
            for e in range(2):
                yo_send(t, e).wait_recv()
                own = wb[t, wrap(y + ways[e]), cuts[e], :].astype(F32)
                ryp[t, e] = (own + ryo[t, e].astype(F32)).astype(BF16)
                yp_send(t, e).start()

    gs = gb[...].reshape(8 * blk, width)

    def product(t):
        with jax.named_scope(f"product waits {t}"):
            for q in range(4):
                xx_own(q, t, 1 - t % 2).wait_recv()
                xx_on(q, t).wait_recv()
        with jax.named_scope(f"product {t}"):
            term = lax.dot_general(
                xb[t].reshape(16 * tok, third), gs, (((0,), (0,)), ((), ())), preferred_element_type=F32
            )
            wb[t] = term.astype(BF16).reshape(wb.shape[1:])
            for e in range(2):
                yo_send(t, e).start()
            for e in range(2):
                yd_send(t, e).start()

    def rza_send(h):
        return remote(sz.at[wrap(j + 2), h], rza.at[h], rza_s.at[h], rza_r.at[h], at_zhi(ways[h]))

    def rzf_send(h):
        way = ways[1 - h]
        return remote(
            sz.at[wrap(j + way), h], rzf.at[1 - h, h], rzf_s.at[1 - h, h], rzf_r.at[1 - h, h], at_zhi(way)
        )

    def sza_send(h):
        return remote(sza.at[h], rzf.at[h, h], rzf_s.at[h, h], rzf_r.at[h, h], at_zhi(ways[h]))

    def input_x():
        with jax.named_scope("input wait x"):
            for kk in range(2):
                pa_send(kk).wait_recv()
                rx_send(kk).wait_recv()
        for q in range(4):
            kk, rows = q // 2, pl.ds((q % 2) * tok, tok)
            total = pb[i * 2 + kk, rows, :].astype(F32)
            for e in range(2):
                total = total + rx[e, kk, rows, :].astype(F32)
            total = total.astype(BF16)
            sz[q, 0] = total[:, :wide]
            sz[q, 1] = total[:, wide:]
        for h in range(2):
            rza_send(h).start()
        for h in range(2):
            rzf_send(h).start()

    def lo_part():
        with jax.named_scope("adapter out"):
            for s in range(1, 4):
                lat_x(s).wait_recv()
            lout = jnp.zeros((RANK, width), F32)
            for row in range(16):
                b, p = row // 2, row % 2
                lout = lout + jnp.dot(
                    lat[row // 4, row % 4, :, :tok],
                    gb[b, p * tok : (p + 1) * tok, :],
                    preferred_element_type=F32,
                )
            lg[1, y] = (SCALE * lout).astype(BF16)
            for s in range(1, 4):
                lg_y(1, s).start()

    def li_part(t):
        with jax.named_scope(f"adapter in {t}"):
            if t == 0:
                lgt_sib().wait_recv()
            lin = jnp.zeros((RANK, third), F32)
            for row in range(16):
                b, p = row // 2, row % 2
                low = lgt[b % 2, b // 2, :, p * LANES : p * LANES + tok]
                lin = lin + jnp.dot(low, xb[t, row], preferred_element_type=F32)
            lg[0, y, :, t * third : (t + 1) * third] = (SCALE * lin).astype(BF16)
            if t == PARTS - 1:
                for s in range(1, 4):
                    lg_y(0, s).start()

    def ag_own(t, e):
        return remote(gw_out.at[t, y], gw_out.at[t, y], ag_s.at[t, e], ag_r.at[t, e], at_y(ways[e]))

    def ag_on(t, e):
        ref = gw_out.at[t, wrap(y - ways[e]), cuts[e]]
        return remote(ref, ref, ag_s.at[t, 2 + e], ag_r.at[t, 2 + e], at_y(ways[e]))

    def sum_y(t):
        with jax.named_scope(f"y sum {t}"):
            for e in range(2):
                yd_send(t, e).wait_recv()
                yp_send(t, e).wait_recv()
            for h in range(2):
                total = wb[t, y, cuts[h], :].astype(F32)
                for e in range(2):
                    total = total + ryf[t, e, h].astype(F32)
                gw_out[t, y, cuts[h], :] = total.astype(BF16)
            for e in range(2):
                ag_own(t, e).start()

    def spread_y(t):
        with jax.named_scope(f"y spread {t}"):
            for e in range(2):
                ag_own(t, e).wait_recv()
                ag_on(t, e).start()

    def pass_z():
        with jax.named_scope("input sums z"):
            for h in range(2):
                rza_send(h).wait_recv()
                sza[h] = (sz[wrap(j + ways[h]), h].astype(F32) + rza[h].astype(F32)).astype(BF16)
                sza_send(h).start()

    product(0)
    act_x(1, 2)
    act_x(2, 2)
    act_z_last(2)
    input_x()
    act_x(3, 1)
    pass_y(0)
    product(1)
    act_x(3, 2)
    sum_y(0)
    product(2)
    pass_y(1)
    pass_z()
    lo_part()
    for t in range(PARTS):
        li_part(t)
    spread_y(0)
    sum_y(1)
    pass_y(2)
    spread_y(1)
    sum_y(2)

    with jax.named_scope("input wait z"):
        for h in range(2):
            rzf_send(h).wait_recv()
            sza_send(h).wait_recv()
    for h in range(2):
        total = sz[j, h].astype(F32)
        for e in range(2):
            total = total + rzf[e, h].astype(F32)
        gi_out[:, h * wide : (h + 1) * wide] = total.astype(BF16)
    with jax.named_scope("adapters wait y"):
        for s in range(1, 4):
            for n in range(2):
                lg_y(n, s).wait_recv()
    for n in range(CUSTOMERS):
        for m, ref in enumerate((li_out, lo_out)):
            acc = jnp.zeros((RANK, width), F32)
            for g in range(4):
                acc = acc + jnp.where(owner[g] == n, lg[m, g].astype(F32), 0.0)
            ref[n] = acc
    spread_y(2)
    with jax.named_scope("y gather"):
        for t in range(PARTS):
            for e in range(2):
                ag_on(t, e).wait_recv()

    with jax.named_scope("sent"):
        for d in range(2):
            for s in range(4):
                sent = (o >= s) if d == 0 else (o <= 3 - s)
                if s < 3:

                    @pl.when(jnp.logical_and(sent, (o < 3) if d == 0 else (o > 0)))
                    def _():
                        for h in range(2):
                            g_hop(d, s, h).wait_send()

                if s > 0 or d == 0:

                    @pl.when(sent)
                    def _():
                        for h in range(2):
                            g_sib(d, s, h).wait_send()

        for t in range(PARTS):
            for e in range(2):
                xz_own(t, e).wait_send()
            xz_on(t).wait_send()
            for q in range(4):
                for e in range(2):
                    xx_own(q, t, e).wait_send()
                xx_on(q, t).wait_send()
            for e in range(2):
                yo_send(t, e).wait_send()
                yd_send(t, e).wait_send()
                yp_send(t, e).wait_send()
                ag_own(t, e).wait_send()
                ag_on(t, e).wait_send()
        for h in range(2):
            ra_send(h).wait_send()
            rx_send(h).wait_send()
            pa_send(h).wait_send()
            rza_send(h).wait_send()
            rzf_send(h).wait_send()
            sza_send(h).wait_send()
        las_send().wait_send()
        lgt_sib().wait_send()
        for s in range(1, 4):
            for small in (lgx_send, lgz_send, laz_send, lgt_send, lat_send, lat_x):
                small(s).wait_send()
            for n in range(2):
                lg_y(n, s).wait_send()


def local(activations, cotangent, preact, weight, ain, aout, owner):
    tok, width = activations.shape
    blk = cotangent.shape[0]
    wide = width // 2
    third = width // PARTS
    piece = third // 4
    hbm = pl.BlockSpec(memory_space=pltpu.HBM)
    dma = pltpu.SemaphoreType.DMA
    v = pltpu.VMEM
    scratch = [
        v((8, blk, width), BF16),
        v((PARTS, 16, tok, third), BF16),
        v((blk, width), BF16),
        v((blk, width), BF16),
        v((width, width), BF16),
        v((CUSTOMERS, RANK, width), BF16),
        v((CUSTOMERS, RANK, width), BF16),
        v((RANK, width), BF16),
        v((RANK, width), BF16),
        v((width, width), BF16),
        v((8, blk, width), BF16),
        v((2, blk, width), BF16),
        v((2, blk, width), BF16),
        v((2, 2, blk, width), BF16),
        v((4, 2, tok, wide), BF16),
        v((2, tok, wide), BF16),
        v((2, tok, wide), BF16),
        v((2, 2, tok, wide), BF16),
        v((PARTS, 4, piece, width), BF16),
        v((PARTS, 2, piece // 2, width), BF16),
        v((PARTS, 2, piece // 2, width), BF16),
        v((PARTS, 2, 2, piece // 2, width), BF16),
        v((4, RANK, 2 * LANES), BF16),
        v((4, RANK, 2 * LANES), BF16),
        v((2, 4, RANK, 2 * LANES), BF16),
        v((2, RANK, LANES), BF16),
        v((4, RANK, LANES), BF16),
        v((4, 4, RANK, LANES), BF16),
        v((2, 4, RANK, width), BF16),
        dma((8,)),
        dma((PARTS, 3)), dma((PARTS, 3)), dma((4, PARTS, 3)), dma((4, PARTS, 3)),
        dma((2, 4, 2)), dma((2, 4, 2)), dma((2, 4, 2)), dma((2, 4, 2)),
        dma((2,)), dma((2,)), dma((2, 2)), dma((2, 2)),
        dma((2,)), dma((2,)), dma((2, 2)), dma((2, 2)),
        dma((PARTS, 2)), dma((PARTS, 2)), dma((PARTS, 2)), dma((PARTS, 2)),
        dma((PARTS, 2)), dma((PARTS, 2)), dma((PARTS, 4)), dma((PARTS, 4)),
        dma((10, 3)), dma((10, 3)),
    ]
    gi, gw, li, lo = pl.pallas_call(
        kernel,
        out_shape=(
            pltpu.VMEM((tok, width), BF16),
            pltpu.VMEM((PARTS, 4, piece, width), BF16),
            pltpu.VMEM((CUSTOMERS, RANK, width), F32),
            pltpu.VMEM((CUSTOMERS, RANK, width), F32),
        ),
        in_specs=[hbm] * 6 + [pl.BlockSpec(memory_space=pltpu.SMEM)],
        out_specs=[pl.BlockSpec(memory_space=pltpu.VMEM)] * 4,
        scratch_shapes=scratch,
        compiler_params=pltpu.CompilerParams(
            collective_id=0, has_side_effects=True, vmem_limit_bytes=60 << 20
        ),
        name="mlp_backward",
    )(activations, cotangent, preact, weight, ain, aout, owner)
    return gi, gw.reshape(width, width), li, lo


def solution(mesh):
    placed = (
        P(("dp", "row"), "col"),
        P(("dp", "col"), "row"),
        P(("dp", "col"), "row"),
        P("col", "row"),
        P(None, None, "col"),
        P(None, None, "row"),
        P(),
    )
    return jax.shard_map(
        local,
        mesh=mesh,
        in_specs=placed,
        out_specs=(
            P(("dp", "row"), "col"),
            P("col", "row"),
            P(None, None, "col"),
            P(None, None, "row"),
        ),
        check_vma=False,
    )
```

time: 136 us -> 121 us (0.89)
  Pallas kernels: 129 us -> 117 us
  local copies, waits for them, and re-layouts: 5.45 us -> 3.11 us
    pallas_call x1, Pallas kernels: 129 us -> 117 us  [local(): pl.pallas_call(kernel, out_shape=(pltpu.VMEM((tok, width), BF16), pltpu.V...]
    unnamed x8 -> x4, local copies, waits for them, and re-layouts: 5.45 us -> 3.11 us
where the time goes in v3:
time: 121 us
  Pallas kernels  117 us (97%)
  local copies, waits for them, and re-layouts  3.11 us (3%)
    pallas_call x1, Pallas kernels, local(): pl.pallas_call(kernel, out_shape=(pltpu.VMEM((tok, width), BF16), pltpu.V...  117 us
    unnamed x4, local copies, waits for them, and re-layouts  3.11 us

profile of v3, /device:TPU:6, one launch (start us, length us, event | category | flops | bytes accessed | tf_op | source)
XLA Modules:
  0.0 121.0 jit_solution(13121505973059238909)
XLA Ops:
  0.6 117.2 %mlp_backward.1 = (bf16[112,768]{1,0:T(8,128)(2,1)S(1)}, bf16[3,4,64,768]{3,2,1,0:T(8,128)(2,1)S(1)}, f32[3,32,768]{2,1,0:T(8,128)S(1)}, f32[3,32,768]{2,1,0:T(8,128)S(1)}) custom-call(bf16[112,768]{1,0:T(8,128)(2,1)} %x_in.1, bf16[224,768]{1,0:T(8,128)(2,1)} %cot_in.1, bf16[224,768]{1,0:T(8,128)(2,1)} %pre_in.1, bf16[768,768]{1,0:T(8,128)(2,1)} %w_in.1, ...), custom_call_target="tpu_custom_call" | custom-call | tf_op jit(solution)/shard_map/mlp_backward/pallas_call | solution.py:641
  117.9 0.7 copy.15
  118.5 1.0 copy.16
  119.5 0.7 copy.17
  120.3 0.7 copy.18

commit v4 on v3

--- a/solution.py
+++ b/solution.py
@@ -14,6 +14,7 @@
 RANK = 32
 LANES = 128
 PARTS = 3
+DIRECT = 3
 
 
 def gelu_slope(v):
@@ -70,7 +71,9 @@
             + [(x_in.at[:, pl.ds(t * third, third)], xb.at[t, r]) for t in range(PARTS)]
         )
     ]
-    for cp in loads:
+    early = [loads[0], loads[1], *loads[5:]]
+    late = loads[2:5]
+    for cp in early:
         cp.start()
     barrier = pltpu.get_barrier_semaphore()
     for s in range(1, 4):
@@ -128,9 +131,15 @@
         row = xrow(i - way, q)
         return remote(xb.at[h, row], xb.at[h, row], xx_s.at[q, h, 2], xx_r.at[q, h, 2], at_x(way))
 
+    def xx_direct(q, h):
+        row = xrow(i, q)
+        return remote(xb.at[h, row], xb.at[h, row], xx_s.at[q, h, 2], xx_r.at[q, h, 2], at_x(2))
+
     def xx_start(q, h):
         for e in range(2):
             xx_own(q, h, e).start()
+        if q == DIRECT:
+            xx_direct(q, h).start()
 
     def xx_forward(q, h):
         xx_own(q, h, h % 2).wait_recv()
@@ -178,6 +187,8 @@
 
     loads[0].wait()
     loads[1].wait()
+    for cp in late:
+        cp.start()
     for h in range(2):
         rows = pl.ds(h * half, half)
         v = prev[rows, :].astype(F32)
@@ -246,38 +257,35 @@
         return (ref[0].astype(F32) + ref[1].astype(F32)) + (ref[2].astype(F32) + ref[3].astype(F32))
 
     def g_step(s):
-        for d in range(2):
-            here = (o >= s) if d == 0 else (o <= 3 - s)
-            oo = wrap(o - s) if d == 0 else wrap(o + s)
-            for h in range(2):
-
-                @pl.when(here)
+        here = (o >= s, o <= 3 - s)
+        more = (o < 3, o > 0)
+        for h in range(2):
+            for d in range(2):
+
+                @pl.when(here[d])
                 def _():
                     g_hop(d, s - 1, h).wait_recv()
 
-                @pl.when(jnp.logical_and(here, (o < 3) if d == 0 else (o > 0)))
+                @pl.when(jnp.logical_and(here[d], more[d]))
                 def _():
                     g_hop(d, s, h).start()
 
-                @pl.when(here)
+                @pl.when(here[d])
                 def _():
                     g_sib(d, s, h).start()
 
-            @pl.when(here)
-            def _():
-                part(oo, k)
-                part_send(oo, k)
-
-        for d in range(2):
-            here = (o >= s) if d == 0 else (o <= 3 - s)
-            oo = wrap(o - s) if d == 0 else wrap(o + s)
-
-            @pl.when(here)
-            def _():
-                for h in range(2):
-                    g_sib(d, s, h).wait_recv()
-                part(oo, 1 - k)
-                part_send(oo, 1 - k)
+        for own in range(2):
+            for d in range(2):
+                oo = wrap(o - s) if d == 0 else wrap(o + s)
+
+                @pl.when(here[d])
+                def _():
+                    kk = k if own == 0 else 1 - k
+                    if own == 1:
+                        for h in range(2):
+                            g_sib(d, s, h).wait_recv()
+                    part(oo, kk)
+                    part_send(oo, kk)
 
     def pass_on(dist):
         with jax.named_scope(f"input sums x {dist}"):
@@ -318,8 +326,19 @@
         act_x(0, t)
     with jax.named_scope("gradients 2"):
         g_step(2)
+    pass_on(1)
+    with jax.named_scope("gradients 3"):
+        g_step(3)
+    with jax.named_scope("gradients out"):
+        for d in range(2):
+
+            @pl.when((o == 2) if d == 0 else (o == 1))
+            def _():
+                for h in range(2):
+                    g_hop(d, 2, h).wait_send()
+
     xz_start(0)
-    pass_on(1)
+    pass_on(2)
     with jax.named_scope("rank stage 2"):
         for s in range(1, 4):
             lgx_send(s).wait_recv()
@@ -329,11 +348,14 @@
         for s in range(1, 4):
             lgz_send(s).start()
             laz_send(s).start()
-    with jax.named_scope("gradients 3"):
-        g_step(3)
+    act_z(0)
     xz_start(1)
-    pass_on(2)
-    act_z(0)
+    pass_on(3)
+    act_x(1, 0)
+    act_x(2, 0)
+    act_z_last(0)
+    act_z(1)
+    xz_start(2)
     with jax.named_scope("rank stage 3"):
         for s in range(1, 4):
             lgz_send(s).wait_recv()
@@ -343,24 +365,11 @@
         for s in range(1, 4):
             lgt_send(s).start()
             lat_send(s).start()
-    xz_start(2)
-    act_x(1, 0)
-    act_x(2, 0)
-    act_z_last(0)
-    act_z(1)
-    pass_on(3)
-    act_x(3, 0)
     act_x(1, 1)
     act_x(2, 1)
+    act_z_last(1)
     act_z(2)
-    act_z_last(1)
-    with jax.named_scope("rank stage 4"):
-        for s in range(1, 4):
-            lgt_send(s).wait_recv()
-            lat_send(s).wait_recv()
-        lgt_sib().start()
-        for s in range(1, 4):
-            lat_x(s).start()
+
     low_rows = wb.shape[2] // 2
     cuts = (pl.ds(0, low_rows), pl.ds(low_rows, low_rows))
 
@@ -390,6 +399,8 @@
     def product(t):
         with jax.named_scope(f"product waits {t}"):
             for q in range(4):
+                if q == DIRECT:
+                    xx_own(q, t, t % 2).wait_recv()
                 xx_own(q, t, 1 - t % 2).wait_recv()
                 xx_on(q, t).wait_recv()
         with jax.named_scope(f"product {t}"):
@@ -429,8 +440,6 @@
             sz[q, 1] = total[:, wide:]
         for h in range(2):
             rza_send(h).start()
-        for h in range(2):
-            rzf_send(h).start()
 
     def lo_part():
         with jax.named_scope("adapter out"):
@@ -494,28 +503,36 @@
                 rza_send(h).wait_recv()
                 sza[h] = (sz[wrap(j + ways[h]), h].astype(F32) + rza[h].astype(F32)).astype(BF16)
                 sza_send(h).start()
+            for h in range(2):
+                rzf_send(h).start()
 
     product(0)
     act_x(1, 2)
     act_x(2, 2)
     act_z_last(2)
     input_x()
-    act_x(3, 1)
     pass_y(0)
     product(1)
-    act_x(3, 2)
+    with jax.named_scope("rank stage 4"):
+        for s in range(1, 4):
+            lgt_send(s).wait_recv()
+            lat_send(s).wait_recv()
+        lgt_sib().start()
+        for s in range(1, 4):
+            lat_x(s).start()
     sum_y(0)
     product(2)
     pass_y(1)
-    pass_z()
     lo_part()
     for t in range(PARTS):
         li_part(t)
+    pass_y(2)
+    sum_y(1)
     spread_y(0)
-    sum_y(1)
-    pass_y(2)
+    pass_z()
+    sum_y(2)
     spread_y(1)
-    sum_y(2)
+    spread_y(2)
 
     with jax.named_scope("input wait z"):
         for h in range(2):
@@ -536,7 +553,6 @@
             for g in range(4):
                 acc = acc + jnp.where(owner[g] == n, lg[m, g].astype(F32), 0.0)
             ref[n] = acc
-    spread_y(2)
     with jax.named_scope("y gather"):
         for t in range(PARTS):
             for e in range(2):
@@ -546,7 +562,7 @@
         for d in range(2):
             for s in range(4):
                 sent = (o >= s) if d == 0 else (o <= 3 - s)
-                if s < 3:
+                if s < 2:
 
                     @pl.when(jnp.logical_and(sent, (o < 3) if d == 0 else (o > 0)))
                     def _():

time: 121 us -> 112 us (0.926); the launches traced: 121 us -> 110 us
  Pallas kernels: 117 us -> 106 us
    pallas_call x1, Pallas kernels: 117 us -> 106 us  [local(): pl.pallas_call(kernel, out_shape=(pltpu.VMEM((tok, width), BF16), pltpu.V...]
where the time goes in v4:
time: 112 us; the launch traced here: 110 us
  Pallas kernels  106 us (95%)
  local copies, waits for them, and re-layouts  3.11 us (3%)
    pallas_call x1, Pallas kernels, local(): pl.pallas_call(kernel, out_shape=(pltpu.VMEM((tok, width), BF16), pltpu.V...  106 us
    unnamed x4, local copies, waits for them, and re-layouts  3.11 us

profile of v4, /device:TPU:6, one launch (start us, length us, event | category | flops | bytes accessed | tf_op | source)
XLA Modules:
  0.0 109.8 jit_solution(285301696621162351)
XLA Ops:
  0.6 106.1 %mlp_backward.1 = (bf16[112,768]{1,0:T(8,128)(2,1)S(1)}, bf16[3,4,64,768]{3,2,1,0:T(8,128)(2,1)S(1)}, f32[3,32,768]{2,1,0:T(8,128)S(1)}, f32[3,32,768]{2,1,0:T(8,128)S(1)}) custom-call(bf16[112,768]{1,0:T(8,128)(2,1)} %x_in.1, bf16[224,768]{1,0:T(8,128)(2,1)} %cot_in.1, bf16[224,768]{1,0:T(8,128)(2,1)} %pre_in.1, bf16[768,768]{1,0:T(8,128)(2,1)} %w_in.1, ...), custom_call_target="tpu_custom_call" | custom-call | tf_op jit(solution)/shard_map/mlp_backward/pallas_call | solution.py:657
  106.7 0.7 copy.15
  107.4 1.0 copy.16
  108.4 0.7 copy.17
  109.1 0.7 copy.18

commit v5 on v4

--- a/solution.py
+++ b/solution.py
@@ -350,12 +350,12 @@
             laz_send(s).start()
     act_z(0)
     xz_start(1)
+    xz_start(2)
     pass_on(3)
     act_x(1, 0)
     act_x(2, 0)
+    act_z(1)
     act_z_last(0)
-    act_z(1)
-    xz_start(2)
     with jax.named_scope("rank stage 3"):
         for s in range(1, 4):
             lgz_send(s).wait_recv()
@@ -367,9 +367,8 @@
             lat_send(s).start()
     act_x(1, 1)
     act_x(2, 1)
+    act_z(2)
     act_z_last(1)
-    act_z(2)
-
     low_rows = wb.shape[2] // 2
     cuts = (pl.ds(0, low_rows), pl.ds(low_rows, low_rows))
 
@@ -454,8 +453,6 @@
                     preferred_element_type=F32,
                 )
             lg[1, y] = (SCALE * lout).astype(BF16)
-            for s in range(1, 4):
-                lg_y(1, s).start()
 
     def li_part(t):
         with jax.named_scope(f"adapter in {t}"):
@@ -467,9 +464,6 @@
                 low = lgt[b % 2, b // 2, :, p * LANES : p * LANES + tok]
                 lin = lin + jnp.dot(low, xb[t, row], preferred_element_type=F32)
             lg[0, y, :, t * third : (t + 1) * third] = (SCALE * lin).astype(BF16)
-            if t == PARTS - 1:
-                for s in range(1, 4):
-                    lg_y(0, s).start()
 
     def ag_own(t, e):
         return remote(gw_out.at[t, y], gw_out.at[t, y], ag_s.at[t, e], ag_r.at[t, e], at_y(ways[e]))
@@ -503,16 +497,12 @@
                 rza_send(h).wait_recv()
                 sza[h] = (sz[wrap(j + ways[h]), h].astype(F32) + rza[h].astype(F32)).astype(BF16)
                 sza_send(h).start()
-            for h in range(2):
-                rzf_send(h).start()
 
     product(0)
     act_x(1, 2)
     act_x(2, 2)
     act_z_last(2)
     input_x()
-    pass_y(0)
-    product(1)
     with jax.named_scope("rank stage 4"):
         for s in range(1, 4):
             lgt_send(s).wait_recv()
@@ -520,17 +510,24 @@
         lgt_sib().start()
         for s in range(1, 4):
             lat_x(s).start()
+    pass_y(0)
+    product(1)
     sum_y(0)
+    for h in range(2):
+        rzf_send(h).start()
     product(2)
     pass_y(1)
+    pass_y(2)
     lo_part()
     for t in range(PARTS):
         li_part(t)
-    pass_y(2)
     sum_y(1)
     spread_y(0)
     pass_z()
     sum_y(2)
+    for n in range(2):
+        for s in range(1, 4):
+            lg_y(n, s).start()
     spread_y(1)
     spread_y(2)
 

time: 112 us -> 112 us (level)
  the two profiles are of different devices: /device:TPU:6 before, /device:TPU:2 now
where the time goes in v5:
time: 112 us
  Pallas kernels  108 us (96%)
  local copies, waits for them, and re-layouts  3.11 us (3%)
    pallas_call x1, Pallas kernels, local(): pl.pallas_call(kernel, out_shape=(pltpu.VMEM((tok, width), BF16), pltpu.V...  108 us
    unnamed x4, local copies, waits for them, and re-layouts  3.11 us

profile of v5, /device:TPU:2, one launch (start us, length us, event | category | flops | bytes accessed | tf_op | source)
XLA Modules:
  0.0 112.0 jit_solution(2489238761203998824)
XLA Ops:
  0.6 108.2 %mlp_backward.1 = (bf16[112,768]{1,0:T(8,128)(2,1)S(1)}, bf16[3,4,64,768]{3,2,1,0:T(8,128)(2,1)S(1)}, f32[3,32,768]{2,1,0:T(8,128)S(1)}, f32[3,32,768]{2,1,0:T(8,128)S(1)}) custom-call(bf16[112,768]{1,0:T(8,128)(2,1)} %x_in.1, bf16[224,768]{1,0:T(8,128)(2,1)} %cot_in.1, bf16[224,768]{1,0:T(8,128)(2,1)} %pre_in.1, bf16[768,768]{1,0:T(8,128)(2,1)} %w_in.1, ...), custom_call_target="tpu_custom_call" | custom-call | tf_op jit(solution)/shard_map/mlp_backward/pallas_call | solution.py:654
  108.9 0.7 copy.15
  109.5 1.0 copy.16
  110.6 0.7 copy.17
  111.3 0.7 copy.18

commit v6 on v5

--- a/solution.py
+++ b/solution.py
@@ -601,6 +601,14 @@
                 small(s).wait_send()
             for n in range(2):
                 lg_y(n, s).wait_send()
+
+
+def store_kernel(*refs):
+    copies = [pltpu.make_async_copy(refs[n], refs[4 + n], refs[8].at[n]) for n in range(4)]
+    for cp in copies:
+        cp.start()
+    for cp in copies:
+        cp.wait()
 
 
 def local(activations, cotangent, preact, weight, ain, aout, owner):
@@ -667,6 +675,20 @@
         ),
         name="mlp_backward",
     )(activations, cotangent, preact, weight, ain, aout, owner)
+    held = [pltpu.with_memory_space_constraint(v, pltpu.VMEM) for v in (gi, gw, li, lo)]
+    gi, gw, li, lo = pl.pallas_call(
+        store_kernel,
+        out_shape=(
+            jax.ShapeDtypeStruct((tok, width), BF16),
+            jax.ShapeDtypeStruct((PARTS, 4, piece, width), BF16),
+            jax.ShapeDtypeStruct((CUSTOMERS, RANK, width), F32),
+            jax.ShapeDtypeStruct((CUSTOMERS, RANK, width), F32),
+        ),
+        in_specs=[pl.BlockSpec(memory_space=pltpu.VMEM)] * 4,
+        out_specs=[hbm] * 4,
+        scratch_shapes=[dma((4,))],
+        name="store_results",
+    )(*held)
     return gi, gw.reshape(width, width), li, lo
 
 

time: 112 us -> 110 us (0.982)
  local copies, waits for them, and re-layouts: 3.11 us -> 0 us
  Pallas kernels: 108 us -> 110 us
    unnamed x4 -> x0, local copies, waits for them, and re-layouts: 3.11 us -> none
    pallas_call x0 -> x1, Pallas kernels: none -> 1.29 us  [local(): pl.pallas_call(store_kernel, out_shape=(jax.ShapeDtypeStruct((tok, width)...]
where the time goes in v6:
time: 110 us
  Pallas kernels  110 us (100%)
    pallas_call x1, Pallas kernels, local(): pl.pallas_call(kernel, out_shape=(pltpu.VMEM((tok, width), BF16), pltpu.V...  108 us

profile of v6, /device:TPU:2, one launch (start us, length us, event | category | flops | bytes accessed | tf_op | source)
XLA Modules:
  0.0 110.3 jit_solution(8787911458185493810)
XLA Ops:
  0.6 108.2 %mlp_backward.1 = (bf16[112,768]{1,0:T(8,128)(2,1)S(1)}, bf16[3,4,64,768]{3,2,1,0:T(8,128)(2,1)S(1)}, f32[3,32,768]{2,1,0:T(8,128)S(1)}, f32[3,32,768]{2,1,0:T(8,128)S(1)}) custom-call(bf16[112,768]{1,0:T(8,128)(2,1)} %x_in.1, bf16[224,768]{1,0:T(8,128)(2,1)} %cot_in.1, bf16[224,768]{1,0:T(8,128)(2,1)} %pre_in.1, bf16[768,768]{1,0:T(8,128)(2,1)} %w_in.1, ...), custom_call_target="tpu_custom_call" | custom-call | tf_op jit(solution)/shard_map/mlp_backward/pallas_call | solution.py:662
  108.9 1.3 %store_results.1 = (bf16[112,768]{1,0:T(8,128)(2,1)}, bf16[3,4,64,768]{3,2,1,0:T(8,128)(2,1)}, f32[3,32,768]{2,1,0:T(8,128)}, f32[3,32,768]{2,1,0:T(8,128)}) custom-call(bf16[112,768]{1,0:T(8,128)(2,1)S(1)} %get-tuple-element.12.refs_0_, bf16[3,4,64,768]{3,2,1,0:T(8,128)(2,1)S(1)} %get-tuple-element.13.refs_1_, f32[3,32,768]{2,1,0:T(8,128)S(1)} %get-tuple-element.14.refs_2_, ...), custom_call_target="tpu_custom_call" | custom-call | tf_op jit(solution)/shard_map/store_results/pallas_call | solution.py:679
